TPU v7x, 256 devices: a whole 4x4x8 slice. The times are simulated.
256 devices in a mesh: req: 4 (over x), seq: 32 (over z, y), tp: 2 (over core).
Axes of the slice: x: 4, y: 4, z: 8, core: 2. Of those that a mesh axis runs over, the one named last changes fastest.
Arguments:
- keys: bfloat16 [4, 32768, 4, 8, 128], P('req', 'seq', None, 'tp'), may hold values from -40 to 40
- start_basis: bfloat16 [4, 4, 8, 128, 256], P('req', None, 'tp'), may hold values from -0.09375 to 0.09375
- owner_map: int32 [4, 32, 16], P('req', 'seq'), may hold values from 0 to 15, each once within a row
Outputs:
- handed: bfloat16 [4, 32, 4, 256, 256], P('req', 'seq')
Inputs may be any that keep to these rules, and one draw needn't show every extreme that they name: Each row owner_map[r, s, :] is a permutation of 0 to 15: block b goes to decode owner owner_map[r, s, b] // 4, slot owner_map[r, s, b] % 4.
All inputs are finite; a program needn't handle non-finite values.
Results may differ from a plain program's by a relative error of at most 0.0085.
Values may be sent and summed in bfloat16 or wider, within the bound.
A program may use at most 64 MiB of HBM per device.

v0:
```python
import jax
import jax.numpy as jnp
from jax import lax
from jax.sharding import PartitionSpec as P

ITERS = 2


def orthonormalize(moment, gram_matrix):
    rank_size = gram_matrix.shape[0]
    shift_value = 0.0001 * jnp.trace(gram_matrix) / rank_size
    shifted = gram_matrix + shift_value * jnp.eye(rank_size, dtype=jnp.float32)
    factor = jnp.linalg.cholesky(shifted)
    return jax.scipy.linalg.solve_triangular(factor, moment.T, lower=True).T


def gram_product(moment):
    return jnp.dot(
        moment.T, moment, precision=lax.Precision.HIGHEST, preferred_element_type=jnp.float32
    )


def sum_heads(partial_value):
    return lax.psum(partial_value, "tp")


def moment_product(key_cols, coefficients):
    return lax.dot_general(
        key_cols, coefficients, (((0,), (0,)), ((), ())), preferred_element_type=jnp.float32
    )


def body(keys, start_basis, owner_map):
    tokens = keys.shape[1]
    columns = start_basis.shape[-1]
    key_rows = keys.reshape(tokens, -1)
    basis_now = start_basis.reshape(key_rows.shape[1], -1)
    partial_value = jnp.dot(key_rows, basis_now, preferred_element_type=jnp.float32)
    for iteration in range(ITERS):
        projected = sum_heads(partial_value).astype(jnp.bfloat16)
        moment = lax.psum(moment_product(key_rows, projected), "seq")
        gram_matrix = lax.psum(gram_product(moment), "tp")
        basis_now = orthonormalize(moment, gram_matrix).astype(jnp.bfloat16)
        partial_value = jnp.dot(key_rows, basis_now, preferred_element_type=jnp.float32)
    coefficients = sum_heads(partial_value).astype(jnp.bfloat16)
    blocks = owner_map.shape[2]
    block_rows = coefficients.reshape(blocks, -1)
    slot_table = (
        owner_map.reshape(1, blocks) == jnp.arange(blocks, dtype=jnp.int32)[:, None]
    ).astype(jnp.bfloat16)
    placed = jnp.dot(slot_table, block_rows, preferred_element_type=jnp.float32).astype(
        jnp.bfloat16
    )
    owners = lax.axis_size("req")
    placed = placed.reshape(owners, -1, columns)
    handed = lax.all_to_all(placed, "req", split_axis=0, concat_axis=0, tiled=True)
    return handed.reshape(1, 1, owners, -1, columns)


def solution(mesh):
    placed = (
        P("req", "seq", None, "tp", None),
        P("req", None, "tp", None, None),
        P("req", "seq", None),
    )
    return jax.shard_map(
        body,
        mesh=mesh,
        in_specs=placed,
        out_specs=P("req", "seq", None, None, None),
        check_vma=False,
    )
```

profile of v0, /device:TPU:1, one launch (start us, length us, event | category | flops | bytes accessed | tf_op | source)
XLA Modules:
  0.0 593.2 jit_solution(12987570884506016273)
XLA Ops:
  6.5 7.9 %reshape.38 = bf16[1024,2048]{1,0:T(8,128)(2,1)} reshape(bf16[1,1024,4,4,128]{4,3,2,1,0:T(4,128)(2,1)} %param.6) | data formatting | bytes 8388608 | tf_op jit(solution)/shard_map/reshape | solution.py:36
  14.4 3.4 fusion.2
  17.9 9.4 %all-reduce.16 = bf16[1024,256]{1,0:T(8,128)(2,1)S(1)} all-reduce(f32[1024,256]{1,0:T(8,128)S(1)} %fusion.2), channel_id=1, replica_groups=mesh['req'=4,'seq'=32,'tp'=2] {'tp'}, use_global_device_ids=true, to_apply=%region_0.0 | all-reduce | flops 262144 | bytes 1572864 | tf_op jit(solution)/shard_map/psum | solution.py:24
  27.3 4.8 convolution_bitcast_fusion.1
  32.1 150.7 %all-reduce.9.cloned.1.call-done = f32[2048,256]{0,1:T(8,128)} async-done(((f32[2048,256]{0,1:T(8,128)}), f32[2048,256]{0,1:T(8,128)}) %all-reduce.9.cloned.1.call-update) | async-done | bytes 2097168 | tf_op jit(solution)/shard_map/psum | solution.py:41
  182.8 4.8 fusion.33
  187.6 0.3 all-reduce.13.cloned.1.call-start
  188.0 30.9 %all-reduce.11.cloned.1.call-done = f32[256,256]{0,1:T(8,128)} async-done(((f32[256,256]{0,1:T(8,128)}), f32[256,256]{0,1:T(8,128)}) %all-reduce.11.cloned.1.call-update) | async-done | bytes 262160 | tf_op jit(solution)/shard_map/psum | solution.py:42
  218.9 1.6 select_reduce_fusion.1
  221.1 1.0 select_add_fusion.1
  222.1 0.8 copy.9
  222.9 1.1 fusion.13
  224.0 0.7 copy-done.7
  224.7 11.7 %cholesky.130 = f32[128,128]{1,0:T(8,128)S(1)} custom-call(f32[128,128]{1,0:T(8,128)S(1)} %cholesky.194), custom_call_target="Cholesky" | custom-call | tf_op jit(solution)/shard_map/jit(cholesky)/cholesky | solution.py:13
  236.5 9.8 %custom-call.13 = f32[1,128,128]{1,2,0:T(8,128)S(1)} custom-call(f32[1,128,128]{2,1,0:T(8,128)S(1)} %get-tuple-element.50), custom_call_target="InvertDiagBlocksLowerTriangular" | custom-call | tf_op jit(solution)/shard_map/jit(cholesky)/cholesky | solution.py:13
  246.3 1.0 constant_dynamic-update-slice_fusion.3
  247.4 1.1 convolution_subtract_fusion.3
  248.5 11.7 %cholesky.147 = f32[128,128]{1,0:T(8,128)S(1)} custom-call(f32[128,128]{1,0:T(8,128)S(1)} %convolution_subtract_fusion.3), custom_call_target="Cholesky" | custom-call | tf_op jit(solution)/shard_map/jit(cholesky)/cholesky | solution.py:13
  260.2 0.7 compare_reduce_fusion.2
  262.1 1.0 select_select_fusion.1
  263.2 4.4 while.4
  263.7 0.6 fusion.56
  264.3 1.3 bitcast_dynamic-update-slice_fusion.4
  265.7 0.6 fusion.56
  266.2 1.3 bitcast_dynamic-update-slice_fusion.4
  267.6 0.6 copy-done.10
  268.2 20.5 %custom-call.14 = f32[2,128,128]{1,2,0:T(8,128)S(1)} custom-call(f32[2,128,128]{2,1,0:T(8,128)} %copy-done.10), custom_call_target="InvertDiagBlocksLowerTriangular" | custom-call | tf_op jit(solution)/shard_map/jit(_solve_triangular)/triangular_solve | solution.py:14
  288.7 1.1 fusion.7
  289.8 1.0 convolution_subtract_fusion.1
  290.8 1.1 fusion.19
  292.0 1.3 convolution_bitcast_fusion.3
  293.3 6.3 %all-reduce.17 = bf16[1024,256]{0,1:T(8,128)(2,1)S(1)} all-reduce(f32[1024,256]{0,1:T(8,128)S(1)} %convolution_bitcast_fusion.3), channel_id=1, replica_groups=mesh['req'=4,'seq'=32,'tp'=2] {'tp'}, use_global_device_ids=true, to_apply=%region_8.11 | all-reduce | flops 262144 | bytes 1572864 | tf_op jit(solution)/shard_map/psum | solution.py:24
  299.6 4.8 convolution_bitcast_fusion
  304.6 150.4 %all-reduce.13.cloned.1.call-done = f32[2048,256]{0,1:T(8,128)} async-done(((f32[2048,256]{0,1:T(8,128)}), f32[2048,256]{0,1:T(8,128)}) %all-reduce.13.cloned.1.call-update) | async-done | bytes 2097168 | tf_op jit(solution)/shard_map/psum | solution.py:41
  455.1 4.8 fusion.34
  459.9 31.2 %all-reduce.15.cloned.1.call-done = f32[256,256]{0,1:T(8,128)} async-done(((f32[256,256]{0,1:T(8,128)}), f32[256,256]{0,1:T(8,128)}) %all-reduce.15.cloned.1.call-update) | async-done | bytes 262160 | tf_op jit(solution)/shard_map/psum | solution.py:42
  491.1 1.6 select_reduce_fusion
  493.4 1.0 select_add_fusion
  494.4 0.8 copy.11
  495.2 1.1 fusion.12
  496.3 0.7 copy-done.8
  497.0 11.7 %cholesky.164 = f32[128,128]{1,0:T(8,128)S(1)} custom-call(f32[128,128]{1,0:T(8,128)S(1)} %cholesky.197), custom_call_target="Cholesky" | custom-call | tf_op jit(solution)/shard_map/jit(cholesky)/cholesky | solution.py:13
  508.8 9.8 %custom-call.15 = f32[1,128,128]{1,2,0:T(8,128)S(1)} custom-call(f32[1,128,128]{2,1,0:T(8,128)S(1)} %get-tuple-element.46), custom_call_target="InvertDiagBlocksLowerTriangular" | custom-call | tf_op jit(solution)/shard_map/jit(cholesky)/cholesky | solution.py:13
  518.6 1.0 constant_dynamic-update-slice_fusion.1
  519.6 1.1 convolution_subtract_fusion.2
  520.7 11.9 %cholesky.181 = f32[128,128]{1,0:T(8,128)S(1)} custom-call(f32[128,128]{1,0:T(8,128)S(1)} %convolution_subtract_fusion.2), custom_call_target="Cholesky" | custom-call | tf_op jit(solution)/shard_map/jit(cholesky)/cholesky | solution.py:13
  532.7 0.7 compare_reduce_fusion
  533.3 0.6 compare_reduce_fusion.1
  535.2 1.0 select_select_fusion
  536.2 3.9 while.5
  536.2 0.6 fusion.57
  536.8 1.3 bitcast_dynamic-update-slice_fusion.5
  538.2 0.6 fusion.57
  538.8 1.3 bitcast_dynamic-update-slice_fusion.5
  540.1 0.6 copy-done.9
  540.7 20.5 %custom-call.16 = f32[2,128,128]{1,2,0:T(8,128)S(1)} custom-call(f32[2,128,128]{2,1,0:T(8,128)} %copy-done.9), custom_call_target="InvertDiagBlocksLowerTriangular" | custom-call | tf_op jit(solution)/shard_map/jit(_solve_triangular)/triangular_solve | solution.py:14
  561.2 1.1 fusion.5
  562.3 1.0 convolution_subtract_fusion
  563.3 1.1 fusion.15
  564.5 1.3 convolution_bitcast_fusion.2
  565.8 6.3 %all-reduce.18 = bf16[1024,256]{0,1:T(8,128)(2,1)S(1)} all-reduce(f32[1024,256]{0,1:T(8,128)S(1)} %convolution_bitcast_fusion.2), channel_id=1, replica_groups=mesh['req'=4,'seq'=32,'tp'=2] {'tp'}, use_global_device_ids=true, to_apply=%region_12.15 | all-reduce | flops 262144 | bytes 1572864 | tf_op jit(solution)/shard_map/psum | solution.py:24
  572.6 0.3 convolution_convert_fusion
  573.1 12.5 %all_to_all.5 = bf16[4,256,256]{2,1,0:T(8,128)(2,1)S(1)} all-to-all(bf16[4,256,256]{2,1,0:T(8,128)(2,1)S(1)} %reshape.40), channel_id=1, replica_groups=mesh['req'=4,'seq'=32,'tp'=2] {'req'}, dimensions={0} | all-to-all | bytes 1048576 | tf_op jit(solution)/shard_map/all_to_all | solution.py:56
  585.6 0.8 copy.54
  (46 shorter events, 1.6 us)
Async XLA Ops:
  6.5 7.9 %copy-start = (bf16[1,4,4,128,256]{4,3,2,1,0:T(8,128)(2,1)S(1)}, bf16[1,4,4,128,256]{4,3,2,1,0:T(8,128)(2,1)}, u32[]{:S(2)}) copy-start(bf16[1,4,4,128,256]{4,3,2,1,0:T(8,128)(2,1)} %param.7) | copy-start | bytes 3145732
  6.5 176.3 %all-reduce.9.cloned.1.call-start = ((), (), s32[]{:S(2)}) async-start(), calls=%async_computation.1 | async-start | bytes 4194304 | tf_op jit(solution)/shard_map/psum | solution.py:41
  32.1 186.8 %all-reduce.11.cloned.1.call-start = ((), (), s32[]{:S(2)}) async-start(), calls=%async_computation.2 | async-start | bytes 524288 | tf_op jit(solution)/shard_map/psum | solution.py:42
  187.6 267.5 %all-reduce.13.cloned.1.call-start = ((), (), s32[]{:S(2)}) async-start(), calls=%async_computation.3 | async-start | bytes 4194304 | tf_op jit(solution)/shard_map/psum | solution.py:41
  222.1 66.6 %copy-start.1 = (f32[2048,256]{0,1:T(8,128)S(1)}, f32[2048,256]{0,1:T(8,128)}, u32[]{:S(2)}) copy-start(f32[2048,256]{0,1:T(8,128)} %all-reduce.9.cloned.1.call-done) | copy-start | bytes 6291460
  224.0 0.7 copy-start.7
  260.2 1.9 copy-start.6
  267.6 0.7 copy-start.10
  289.8 2.2 copy-start.3
  304.4 186.7 %all-reduce.15.cloned.1.call-start = ((), (), s32[]{:S(2)}) async-start(), calls=%async_computation.4 | async-start | bytes 524288 | tf_op jit(solution)/shard_map/psum | solution.py:42
  494.4 66.9 %copy-start.2 = (f32[2048,256]{0,1:T(8,128)S(1)}, f32[2048,256]{0,1:T(8,128)}, u32[]{:S(2)}) copy-start(f32[2048,256]{0,1:T(8,128)} %all-reduce.13.cloned.1.call-done) | copy-start | bytes 6291460
  496.3 0.7 copy-start.8
  532.7 2.5 copy-start.5
  540.1 0.7 copy-start.9
  562.3 2.2 copy-start.4
  565.8 6.8 %copy-start.11 = (s32[1,1,16]{2,1,0:T(1,128)S(1)}, s32[1,1,16]{2,1,0:T(1,128)}, u32[]{:S(2)}) copy-start(s32[1,1,16]{2,1,0:T(1,128)} %param.8) | copy-start | bytes 196
Sparse Core Ops, SparseCore 0:
  32.2 150.5 all-reduce.8
  187.7 31.0 all-reduce.10
  304.5 150.4 all-reduce.12
  460.0 31.0 all-reduce.14
where the time goes:
time: 598 us; the launch traced here: 593 us
  waiting for transfers between devices  363 us (61%)
  other arithmetic  119 us (20%)
  matrix products  36 us (6%)
  blocking collectives  34.6 us (6%)
  local copies, waits for them, and re-layouts  21.7 us (4%)
  between operations  17.4 us (3%)
    psum x2, waiting for transfers between devices, body(): moment = lax.psum(moment_product(key_rows, projected), 'seq')  301 us
    another operation x13, other arithmetic, orthonormalize(): factor = jnp.linalg.cholesky(shifted)  68.8 us
    psum x2, waiting for transfers between devices, body(): gram_matrix = lax.psum(gram_product(moment), 'tp')  62.1 us
    another operation x5, other arithmetic, orthonormalize(): return jax.scipy.linalg.solve_triangular(factor, moment.T, lower=True).T  42.9 us
    psum x3, blocking collectives, sum_heads(): return lax.psum(partial_value, 'tp')  22.1 us
    all_to_all x1, blocking collectives, body(): lax.all_to_all(placed, 'req', split_axis=0, concat_axis=0, tiled=True)  12.5 us
  transfers between devices with their start and end apart: 4, of which 4 were waited for; matrix products, arithmetic and copies ran while one was open for 0% of the time, Pallas kernels for 0%

commit v1 on v0

v1 whole, which is shorter than its diff:
```python
import functools

import jax
import jax.numpy as jnp
from jax import lax
from jax.experimental import pallas as pl
from jax.experimental.pallas import tpu as pltpu
from jax.sharding import PartitionSpec as P

MESH = pl.DeviceIdType.MESH
HI = lax.Precision.HIGHEST
F32 = jnp.float32
B16 = jnp.bfloat16
YS, ZS = 4, 8
TILE = 256


def dot_nt(a, b, precision=None):
    return lax.dot_general(
        a, b, (((1,), (1,)), ((), ())), precision=precision, preferred_element_type=F32
    )


def dot_tn(a, b, precision=None):
    return lax.dot_general(
        a, b, (((0,), (0,)), ((), ())), precision=precision, preferred_element_type=F32
    )


def eliminate(block):
    b = block.shape[0]
    low = block
    done = []
    for p in range(b // 8):
        height = low.shape[0]
        row = lax.broadcasted_iota(jnp.int32, (height, 128), 0)
        cols = [
            jnp.broadcast_to(low[:, 8 * p + j : 8 * p + j + 1], (height, 128)) for j in range(8)
        ]
        diag = jnp.ones((8, 128), F32)
        for j in range(8):
            pivot = jnp.broadcast_to(cols[j][j : j + 1, :], (8, 128))
            guess = pl.reciprocal(pivot, approx=True)
            inverse = guess * (2.0 - pivot * guess)
            diag = jnp.where(row[:8] == j, pivot, diag)
            factor = cols[j] * jnp.broadcast_to(inverse[:1], (height, 128))
            factor = jnp.where(row > j, factor, 0.0)
            low = low - factor * jnp.broadcast_to(low[j : j + 1, :], (height, 128))
            for m in range(j + 1, 8):
                cols[m] = cols[m] - factor * jnp.broadcast_to(
                    cols[m][j : j + 1, :], (height, 128)
                )
        done.append(low[:8] * lax.rsqrt(diag))
        low = low[8:]
    return jnp.concatenate(done, axis=0)[:, b:]


def invert_factor(gram, out, state):
    n = gram.shape[0]
    b = 64
    r = lax.broadcasted_iota(jnp.int32, (n, n), 0)
    c = lax.broadcasted_iota(jnp.int32, (n, n), 1)
    shift = 0.0001 * jnp.sum(jnp.where(r == c, gram, 0.0)) / n
    state[...] = jnp.where(r == c, gram + shift, gram)
    eye = jnp.where(r[:b, :b] == c[:b, :b], 1.0, 0.0).astype(F32)
    for step in range(n // b):
        lo, hi = step * b, (step + 1) * b
        band = state[lo:hi, :]
        inverse = eliminate(jnp.concatenate([band[:, lo:hi], eye], axis=1))
        parts = ([band[:, :lo]] if lo else []) + [eye] + ([band[:, hi:]] if hi < n else [])
        x = jnp.dot(
            inverse, jnp.concatenate(parts, axis=1), precision=HI, preferred_element_type=F32
        )
        out[lo:hi, :] = jnp.where(c[lo:hi, :] < hi, x, 0.0)
        if hi < n:
            rest = state[hi:, :]
            lane = c[hi:, :]
            rest = jnp.where((lane >= lo) & (lane < hi), 0.0, rest)
            state[hi:, :] = rest - dot_tn(x[:, hi:], x, precision=HI)


def factor_kernel(g_ref, out_ref, state):
    invert_factor(g_ref[...], out_ref, state)


def factor_call(gram):
    n = gram.shape[0]
    return pl.pallas_call(
        factor_kernel,
        out_shape=jax.ShapeDtypeStruct((n, n), F32),
        scratch_shapes=[pltpu.VMEM((n, n), F32)],
        name="factor",
    )(gram)


class Links:
    def __init__(self, send, recv):
        self.send, self.recv, self.count = send, recv, 0

    def copy(self, src, dst, **device):
        i = self.count
        self.count += 1
        return pltpu.make_async_remote_copy(
            src_ref=src,
            dst_ref=dst,
            send_sem=self.send.at[i],
            recv_sem=self.recv.at[i],
            device_id=device,
            device_id_type=MESH,
        )


def greet(partners):
    barrier = pltpu.get_barrier_semaphore()
    for device in partners:
        pl.semaphore_signal(barrier, inc=1, device_id=device, device_id_type=MESH)
    pl.semaphore_wait(barrier, len(partners))


def moment_kernel(first, *refs):
    if first:
        k, basis = refs[:2]
    else:
        k, pin, winv = refs[:3]
    refs = refs[2 if first else 3 :]
    (
        pout, gout, p_own, p_in, z_in, zt, opp, in_a, in_b, right32, left32, right16, left16,
        from_left, from_right, own, zsend, zin, full, g_own, g_in, send, recv,
    ) = refs
    s = lax.axis_index("seq")
    c = lax.axis_index("tp")
    y, z = s % YS, s // YS
    links = Links(send, recv)

    def at_y(d):
        return z * YS + (y + d) % YS

    def at_z(d):
        return ((z + d) % ZS) * YS + y

    greet(
        [{"tp": 1 - c}]
        + [{"seq": at_y(d)} for d in range(1, YS)]
        + [{"seq": at_z(d)} for d in range(1, ZS)]
    )
    tokens = k.shape[0]
    tiles = tokens // TILE

    if first:
        swaps = []
        for i in range(tiles):
            rows = pl.ds(i * TILE, TILE)
            p_own[rows, :] = jnp.dot(k[rows, :], basis[...], preferred_element_type=F32)
            copy = links.copy(p_own.at[rows], z_in.at[rows], tp=1 - c)
            copy.start()
            swaps.append(copy)
        for i in range(tiles):
            rows = pl.ds(i * TILE, TILE)
            swaps[i].wait_recv()
            zt[:, rows] = (p_own[rows, :] + z_in[rows, :]).T.astype(B16)
        for copy in swaps:
            copy.wait_send()
    else:
        for i in range(tiles):
            rows = pl.ds(i * TILE, TILE)
            zt[:, rows] = dot_nt(winv[...], pin[rows, :], precision=HI).astype(B16)

    def quarter(q):
        groups = []
        for t in range(2):
            cols = pl.ds(pl.multiple_of(q * 512 + t * 256, 256), 256)
            product = jnp.dot(zt[...], k[:, cols], preferred_element_type=F32)
            groups += [product[:, :128], product[:, 128:]]
        return groups

    a, b = pl.ds(0, 2), pl.ds(2, 2)
    right, left = at_y(1), at_y(3)
    for g, value in enumerate(quarter((y + 2) % YS)):
        opp[g] = value.astype(B16)
    r1 = links.copy(opp.at[a], in_a, seq=right)
    l1 = links.copy(opp.at[b], in_b, seq=left)
    r1.start()
    l1.start()
    for g, value in enumerate(quarter((y + 1) % YS)):
        if g < 2:
            right32[g] = value
        else:
            right16[g] = value.astype(B16)
    r2b = links.copy(right16.at[b], from_left.at[b], seq=right)
    r2b.start()
    for g, value in enumerate(quarter((y + 3) % YS)):
        if g < 2:
            left16[g] = value.astype(B16)
        else:
            left32[g - 2] = value
    l2a = links.copy(left16.at[a], from_right.at[a], seq=left)
    l2a.start()
    for g, value in enumerate(quarter(y)):
        own[g] = value
    r1.wait_recv()
    right16[a] = (right32[...] + in_a[...].astype(F32)).astype(B16)
    r2a = links.copy(right16.at[a], from_left.at[a], seq=right)
    r2a.start()
    l1.wait_recv()
    left16[b] = (left32[...] + in_b[...].astype(F32)).astype(B16)
    l2b = links.copy(left16.at[b], from_right.at[b], seq=left)
    l2b.start()
    r2b.wait_recv()
    l2b.wait_recv()
    own[b] = own[b] + from_left[b].astype(F32) + from_right[b].astype(F32)
    r2a.wait_recv()
    l2a.wait_recv()
    own[a] = own[a] + from_left[a].astype(F32) + from_right[a].astype(F32)

    for piece in range(ZS):
        zsend[piece] = own[piece // 2, 128 * (piece % 2) : 128 * (piece % 2) + 128, :].astype(B16)
    scatter = []
    for d in (4, 3, 5, 2, 6, 1, 7):
        copy = links.copy(zsend.at[(z + d) % ZS], zin.at[d - 1], seq=at_z(d))
        copy.start()
        scatter.append(copy)
    total = own[z // 2, pl.ds(pl.multiple_of((z % 2) * 128, 128), 128), :]
    for copy in scatter:
        copy.wait_recv()
    for d in range(1, ZS):
        total = total + zin[d - 1].astype(F32)
    full[y, z] = total.astype(B16)
    gather = []
    for d in (4, 3, 5, 2, 6, 1, 7):
        copy = links.copy(full.at[y, z], full.at[y, z], seq=at_z(d))
        copy.start()
        gather.append(copy)
    for copy in [r1, l1, r2b, l2a, r2a, l2b] + scatter:
        copy.wait_send()
    for copy in gather:
        copy.wait_recv()

    a, b = pl.ds(0, 4), pl.ds(4, 4)
    yl, yr, yo = (y + 3) % YS, (y + 1) % YS, (y + 2) % YS

    def pass_on(q, half, to):
        copy = links.copy(full.at[q, half], full.at[q, half], seq=to)
        copy.start()
        return copy

    ra, lb = pass_on(y, a, right), pass_on(y, b, left)
    rb, la = pass_on(y, b, right), pass_on(y, a, left)

    def absorb(q, start):
        groups = [
            jnp.concatenate([full[q, 2 * g], full[q, 2 * g + 1]], axis=0) for g in range(4)
        ]
        block = jnp.concatenate(groups, axis=1)
        cols = pl.ds(pl.multiple_of(q * 512, 512), 512)
        product = dot_nt(block, block)
        g_own[...] = product if start else g_own[...] + product
        for i in range(tiles):
            rows = pl.ds(i * TILE, TILE)
            product = dot_nt(k[rows, cols], block)
            p_own[rows, :] = product if start else p_own[rows, :] + product

    absorb(y, True)
    ra.wait_recv()
    fa = pass_on(yl, a, right)
    lb.wait_recv()
    fb = pass_on(yr, b, left)
    rb.wait_recv()
    absorb(yl, False)
    la.wait_recv()
    absorb(yr, False)
    fa.wait_recv()
    fb.wait_recv()
    absorb(yo, False)

    swap = links.copy(g_own, g_in, tp=1 - c)
    swap.start()
    swaps = []
    for i in range(tiles):
        rows = pl.ds(i * TILE, TILE)
        copy = links.copy(p_own.at[rows], p_in.at[rows], tp=1 - c)
        copy.start()
        swaps.append(copy)
    swap.wait_recv()
    gout[...] = g_own[...] + g_in[...]
    for i in range(tiles):
        rows = pl.ds(i * TILE, TILE)
        swaps[i].wait_recv()
        pout[rows, :] = p_own[rows, :] + p_in[rows, :]
    for copy in gather + [ra, rb, la, lb, fa, fb, swap] + swaps:
        copy.wait_send()


def moment_call(first, keys, *args):
    tokens = keys.shape[0]
    vm = pltpu.VMEM
    return pl.pallas_call(
        functools.partial(moment_kernel, first),
        out_shape=(
            jax.ShapeDtypeStruct((tokens, 256), F32),
            jax.ShapeDtypeStruct((256, 256), F32),
        ),
        in_specs=[pl.BlockSpec(memory_space=vm)] * (1 + len(args)),
        out_specs=(pl.BlockSpec(memory_space=vm),) * 2,
        scratch_shapes=[
            vm((tokens, 256), F32),
            vm((tokens, 256), F32),
            vm((tokens if first else 8, 256), F32),
            vm((256, tokens), B16),
            vm((4, 256, 128), B16),
            vm((2, 256, 128), B16),
            vm((2, 256, 128), B16),
            vm((2, 256, 128), F32),
            vm((2, 256, 128), F32),
            vm((4, 256, 128), B16),
            vm((4, 256, 128), B16),
            vm((4, 256, 128), B16),
            vm((4, 256, 128), B16),
            vm((4, 256, 128), F32),
            vm((8, 128, 128), B16),
            vm((7, 128, 128), B16),
            vm((4, 8, 128, 128), B16),
            vm((256, 256), F32),
            vm((256, 256), F32),
            pltpu.SemaphoreType.DMA((40,)),
            pltpu.SemaphoreType.DMA((40,)),
        ],
        compiler_params=pltpu.CompilerParams(
            collective_id=0 if first else 1,
            has_side_effects=True,
            vmem_limit_bytes=40 * 2**20,
        ),
        name="moment_first" if first else "moment_next",
    )(keys, *args)


def hand_kernel(order, p, winv, out, coef, outbox, halves, send, recv):
    x = lax.axis_index("req")
    c = lax.axis_index("tp")
    links = Links(send, recv)
    greet([{"tp": 1 - c}] + [{"req": (x + d) % 4} for d in range(1, 4)])
    tokens = p.shape[0]
    half = winv[pl.ds(pl.multiple_of(c * 128, 128), 128), :]
    for i in range(tokens // TILE):
        rows = pl.ds(i * TILE, TILE)
        rounded = dot_nt(p[rows, :], half, precision=HI).astype(B16)
        for b in range(TILE // 64):
            coef[i * (TILE // 64) + b] = rounded[64 * b : 64 * b + 64, :]
    for slot in range(16):
        outbox[slot // 4, 64 * (slot % 4) : 64 * (slot % 4) + 64, :] = coef[order[slot]]
    away = []
    for d in (2, 1, 3):
        o = (x + d) % 4
        copy = links.copy(outbox.at[o], halves.at[c, x], req=o)
        copy.start()
        away.append((d, copy))
    halves[c, x] = outbox[x]
    across = []

    def cross(r):
        copy = links.copy(halves.at[c, r], halves.at[c, r], tp=1 - c)
        copy.start()
        across.append(copy)

    cross(x)
    for d, copy in away:
        copy.wait_recv()
        cross((x + 4 - d) % 4)
    for copy in across:
        copy.wait_recv()
    for r in range(4):
        out[r, :, :128] = halves[0, r]
        out[r, :, 128:] = halves[1, r]
    for _, copy in away:
        copy.wait_send()
    for copy in across:
        copy.wait_send()


def hand_call(order, p, winv):
    tokens = p.shape[0]
    vm = pltpu.VMEM
    return pl.pallas_call(
        hand_kernel,
        out_shape=jax.ShapeDtypeStruct((4, 256, 256), B16),
        in_specs=[pl.BlockSpec(memory_space=pltpu.SMEM)] + [pl.BlockSpec(memory_space=vm)] * 2,
        out_specs=pl.BlockSpec(memory_space=vm),
        scratch_shapes=[
            vm((16, 64, 128), B16),
            vm((4, 256, 128), B16),
            vm((2, 4, 256, 128), B16),
            pltpu.SemaphoreType.DMA((8,)),
            pltpu.SemaphoreType.DMA((8,)),
        ],
        compiler_params=pltpu.CompilerParams(
            collective_id=2, has_side_effects=True, vmem_limit_bytes=16 * 2**20
        ),
        name="hand",
    )(order, p, winv)


def body(keys, start_basis, owner_map):
    tokens = keys.shape[1]
    key_rows = keys.reshape(tokens, -1)
    basis = start_basis.reshape(key_rows.shape[1], -1)
    owners = owner_map.reshape(-1)
    slots = jnp.arange(owners.shape[0], dtype=jnp.int32)
    order = jnp.sum(jnp.where(owners[None, :] == slots[:, None], slots[None, :], 0), axis=1)
    p, gram = moment_call(True, key_rows, basis)
    winv = factor_call(gram)
    p, gram = moment_call(False, key_rows, p, winv)
    winv = factor_call(gram)
    handed = hand_call(order, p, winv)
    return handed[None, None]


def solution(mesh):
    placed = (
        P("req", "seq", None, "tp", None),
        P("req", None, "tp", None, None),
        P("req", "seq", None),
    )
    return jax.shard_map(
        body,
        mesh=mesh,
        in_specs=placed,
        out_specs=P("req", "seq", None, None, None),
        check_vma=False,
    )
```

time: 598 us -> 153 us (0.26)
  waiting for transfers between devices: 363 us -> 0 us
  Pallas kernels: 0 us -> 136 us
  other arithmetic: 119 us -> 0.11 us
  matrix products: 36 us -> 0 us
  blocking collectives: 34.6 us -> 0 us
  between operations: 17.4 us -> 0.05 us
    psum x4 -> x0, waiting for transfers between devices: 363 us -> none  [the longest x2 301 us: body(): moment = lax.psum(moment_product(key_rows, projected), 'seq')]
    pallas_call x0 -> x5, Pallas kernels: none -> 136 us  [the longest x2 101 us: moment_call(): pl.pallas_call(functools.partial(moment_kernel, first), out_shape=(jax.Sh...]
    another operation x18 -> x0, other arithmetic: 112 us -> none  [the longest x13 68.8 us: orthonormalize(): factor = jnp.linalg.cholesky(shifted)]
    dot_general x8 -> x0, matrix products: 25.4 us -> none  [the longest x2 9.59 us: moment_product(): lax.dot_general(key_cols, coefficients, (((0,), (0,)), ((), ())), preferr...]
    psum x3 -> x0, blocking collectives: 22.1 us -> none  [sum_heads(): return lax.psum(partial_value, 'tp')]
    all_to_all x1 -> x0, blocking collectives: 12.5 us -> none  [body(): lax.all_to_all(placed, 'req', split_axis=0, concat_axis=0, tiled=True)]
    another operation x10 -> x0, matrix products: 10.5 us -> none  [the longest x6 6.23 us: orthonormalize(): return jax.scipy.linalg.solve_triangular(factor, moment.T, lower=True).T]
    another operation x19 -> x0, local copies, waits for them, and re-layouts: 7.75 us -> none  [the longest x15 7.7 us: orthonormalize(): return jax.scipy.linalg.solve_triangular(factor, moment.T, lower=True).T]
  transfers between devices with their start and end apart: 4 -> 0, of which waited for: 4 -> 0; matrix products, arithmetic and copies ran while one was open for 0% -> 0% of each run, Pallas kernels for 0% -> 0%
where the time goes in v1:
time: 153 us
  Pallas kernels  136 us (89%)
  local copies, waits for them, and re-layouts  16.3 us (11%)
    pallas_call x2, Pallas kernels, moment_call(): pl.pallas_call(functools.partial(moment_kernel, first), out_shape=(jax.Sh...  101 us
    pallas_call x2, Pallas kernels, factor_call(): pl.pallas_call(factor_kernel, out_shape=jax.ShapeDtypeStruct((n, n), F32)...  25.2 us
    pallas_call x1, Pallas kernels, hand_call(): pl.pallas_call(hand_kernel, out_shape=jax.ShapeDtypeStruct((4, 256, 256),...  10.4 us
    unnamed x17, local copies, waits for them, and re-layouts  8.47 us
    reshape x1, local copies, waits for them, and re-layouts, body(): key_rows = keys.reshape(tokens, -1)  7.85 us

profile of v1, /device:TPU:1, one launch (start us, length us, event | category | flops | bytes accessed | tf_op | source)
XLA Modules:
  0.0 152.9 jit_solution(14208152032470035542)
XLA Ops:
  0.0 0.0 copy-start.2
  0.0 7.9 %reshape.7.refs_0_ = bf16[1024,2048]{1,0:T(8,128)(2,1)} reshape(bf16[1,1024,4,4,128]{4,3,2,1,0:T(4,128)(2,1)} %param.3) | data formatting | bytes 8388608 | tf_op jit(solution)/shard_map/reshape | solution.py:403
  7.9 0.0 copy-done.2
  7.9 0.0 copy-start
  7.9 2.2 %copy-done = bf16[1024,2048]{1,0:T(8,128)(2,1)S(1)} copy-done((bf16[1024,2048]{1,0:T(8,128)(2,1)S(1)}, bf16[1024,2048]{1,0:T(8,128)(2,1)}, u32[]{:S(2)}) %copy-start) | copy-done | bytes 4194328
  10.0 54.1 %moment_first.1 = (f32[1024,256]{1,0:T(8,128)S(1)}, f32[256,256]{1,0:T(8,128)S(1)}) custom-call(bf16[1024,2048]{1,0:T(8,128)(2,1)S(1)} %copy-done, bf16[2048,256]{1,0:T(8,128)(2,1)S(1)} %bitcast.4), custom_call_target="tpu_custom_call" | custom-call | tf_op jit(solution)/shard_map/moment_first/pallas_call | solution.py:296
  64.2 0.0 copy-start.6
  64.2 0.7 copy-done.6
  64.9 0.0 copy-start.7
  64.9 12.6 %factor.2.refs_2_ = f32[256,256]{1,0:T(8,128)} custom-call(f32[256,256]{1,0:T(8,128)} %copy-done.6), custom_call_target="tpu_custom_call" | custom-call | tf_op jit(solution)/shard_map/factor/pallas_call | solution.py:88
  77.5 0.0 copy-start.1
  77.5 2.2 %copy-done.1 = bf16[1024,2048]{1,0:T(8,128)(2,1)S(1)} copy-done((bf16[1024,2048]{1,0:T(8,128)(2,1)S(1)}, bf16[1024,2048]{1,0:T(8,128)(2,1)}, u32[]{:S(2)}) %copy-start.1) | copy-done | bytes 4194328
  79.7 0.0 copy-start.4
  79.7 0.9 copy-done.4
  80.6 46.7 %moment_next.1 = (f32[1024,256]{1,0:T(8,128)S(1)}, f32[256,256]{1,0:T(8,128)S(1)}) custom-call(bf16[1024,2048]{1,0:T(8,128)(2,1)S(1)} %copy-done.1, f32[1024,256]{1,0:T(8,128)S(1)} %get-tuple-element.9.refs_1_, f32[256,256]{1,0:T(8,128)S(1)} %copy-done.4), custom_call_target="tpu_custom_call" | custom-call | tf_op jit(solution)/shard_map/moment_next/pallas_call | solution.py:296
  127.3 0.0 copy-start.5
  127.4 0.7 copy-done.5
  128.1 12.6 %factor.3.winv = f32[256,256]{1,0:T(8,128)} custom-call(f32[256,256]{1,0:T(8,128)} %copy-done.5), custom_call_target="tpu_custom_call" | custom-call | tf_op jit(solution)/shard_map/factor/pallas_call | solution.py:88
  140.7 0.0 copy-done.7
  140.7 0.1 select_reduce_fusion.order
  140.8 0.0 copy-start.3
  140.8 0.9 copy-done.3
  141.7 10.4 %hand.1 = bf16[4,256,256]{2,1,0:T(8,128)(2,1)S(1)} custom-call(s32[16]{0:T(128)S(1)} %select_reduce_fusion.order, f32[1024,256]{1,0:T(8,128)S(1)} %get-tuple-element.11.p, f32[256,256]{1,0:T(8,128)S(1)} %copy-done.3), custom_call_target="tpu_custom_call" | custom-call | tf_op jit(solution)/shard_map/hand/pallas_call | solution.py:382
  152.1 0.8 copy.5
Async XLA Ops:
  0.0 7.9 %copy-start.2 = (bf16[1,4,4,128,256]{4,3,2,1,0:T(8,128)(2,1)S(1)}, bf16[1,4,4,128,256]{4,3,2,1,0:T(8,128)(2,1)}, u32[]{:S(2)}) copy-start(bf16[1,4,4,128,256]{4,3,2,1,0:T(8,128)(2,1)} %param.4) | copy-start | bytes 3145732
  7.9 2.2 %copy-start = (bf16[1024,2048]{1,0:T(8,128)(2,1)S(1)}, bf16[1024,2048]{1,0:T(8,128)(2,1)}, u32[]{:S(2)}) copy-start(bf16[1024,2048]{1,0:T(8,128)(2,1)} %reshape.7.refs_0_) | copy-start | bytes 12582916
  64.2 0.7 copy-start.6
  64.9 75.8 %copy-start.7 = (s32[1,1,16]{2,1,0:T(1,128)S(1)}, s32[1,1,16]{2,1,0:T(1,128)}, u32[]{:S(2)}) copy-start(s32[1,1,16]{2,1,0:T(1,128)} %param.5) | copy-start | bytes 196
  77.5 2.2 %copy-start.1 = (bf16[1024,2048]{1,0:T(8,128)(2,1)S(1)}, bf16[1024,2048]{1,0:T(8,128)(2,1)}, u32[]{:S(2)}) copy-start(bf16[1024,2048]{1,0:T(8,128)(2,1)} %reshape.7.refs_0_) | copy-start | bytes 12582916
  79.7 0.9 copy-start.4
  127.3 0.7 copy-start.5
  140.8 1.0 copy-start.3

commit v2 on v0

v2 whole, which is shorter than its diff:
```python
import jax
import jax.numpy as jnp
from jax import lax
from jax.experimental import pallas as pl
from jax.experimental.pallas import tpu as pltpu
from jax.sharding import PartitionSpec as P

MESH = pl.DeviceIdType.MESH
HI = lax.Precision.HIGHEST
F32 = jnp.float32
B16 = jnp.bfloat16
YS, ZS = 4, 8
ITERS = 2
TILE = 256
FEATS = 128
CHUNKS = 4
PIECE = 256 // ZS


def dot_nt(a, b, precision=None):
    return lax.dot_general(
        a, b, (((1,), (1,)), ((), ())), precision=precision, preferred_element_type=F32
    )


def dot_tn(a, b, precision=None):
    return lax.dot_general(
        a, b, (((0,), (0,)), ((), ())), precision=precision, preferred_element_type=F32
    )


def eliminate(block):
    b = block.shape[0]
    low = block
    done = []
    for p in range(b // 8):
        height = low.shape[0]
        row = lax.broadcasted_iota(jnp.int32, (height, 128), 0)
        cols = [
            jnp.broadcast_to(low[:, 8 * p + j : 8 * p + j + 1], (height, 128)) for j in range(8)
        ]
        diag = jnp.ones((8, 128), F32)
        for j in range(8):
            pivot = jnp.broadcast_to(cols[j][j : j + 1, :], (8, 128))
            guess = pl.reciprocal(pivot, approx=True)
            inverse = guess * (2.0 - pivot * guess)
            diag = jnp.where(row[:8] == j, pivot, diag)
            factor = cols[j] * jnp.broadcast_to(inverse[:1], (height, 128))
            factor = jnp.where(row > j, factor, 0.0)
            low = low - factor * jnp.broadcast_to(low[j : j + 1, :], (height, 128))
            for m in range(j + 1, 8):
                cols[m] = cols[m] - factor * jnp.broadcast_to(
                    cols[m][j : j + 1, :], (height, 128)
                )
        done.append(low[:8] * lax.rsqrt(diag))
        low = low[8:]
    return jnp.concatenate(done, axis=0)[:, b:]


def invert_factor(gram, out, state):
    n = gram.shape[0]
    b = 64
    r = lax.broadcasted_iota(jnp.int32, (n, n), 0)
    c = lax.broadcasted_iota(jnp.int32, (n, n), 1)
    shift = 0.0001 * jnp.sum(jnp.where(r == c, gram, 0.0)) / n
    state[...] = jnp.where(r == c, gram + shift, gram)
    eye = jnp.where(r[:b, :b] == c[:b, :b], 1.0, 0.0).astype(F32)
    for step in range(n // b):
        lo, hi = step * b, (step + 1) * b
        band = state[lo:hi, :]
        inverse = eliminate(jnp.concatenate([band[:, lo:hi], eye], axis=1))
        parts = ([band[:, :lo]] if lo else []) + [eye] + ([band[:, hi:]] if hi < n else [])
        x = jnp.dot(
            inverse, jnp.concatenate(parts, axis=1), precision=HI, preferred_element_type=F32
        )
        out[lo:hi, :] = jnp.where(c[lo:hi, :] < hi, x, 0.0)
        if hi < n:
            rest = state[hi:, :]
            lane = c[hi:, :]
            rest = jnp.where((lane >= lo) & (lane < hi), 0.0, rest)
            state[hi:, :] = rest - dot_tn(x[:, hi:], x, precision=HI)


class Links:
    def __init__(self, send, recv):
        self.send, self.recv, self.count, self.open = send, recv, 0, []

    def start(self, src, dst, **device):
        i = self.count
        self.count += 1
        copy = pltpu.make_async_remote_copy(
            src_ref=src,
            dst_ref=dst,
            send_sem=self.send.at[i],
            recv_sem=self.recv.at[i],
            device_id=device,
            device_id_type=MESH,
        )
        copy.start()
        self.open.append(copy)
        return copy

    def drain(self):
        for copy in self.open:
            copy.wait_send()
        self.open = []


def greet(partners):
    barrier = pltpu.get_barrier_semaphore()
    for device in partners:
        pl.semaphore_signal(barrier, inc=1, device_id=device, device_id_type=MESH)
    pl.semaphore_wait(barrier, len(partners))


COPIES = 4 + ITERS * (CHUNKS * (6 + 14 + 6) + 1 + 4) + 7


def subspace_kernel(
    order, keys, basis, out,
    raw, k, v0, zt, p_own, z_in, p_in, opp, right32, left32, right16, left16, own, zsend,
    in_a, in_b, from_left, from_right, zin, full, g_own, g_in, state, winv,
    coef, outbox, halves, load, send, recv,
):
    x = lax.axis_index("req")
    s = lax.axis_index("seq")
    c = lax.axis_index("tp")
    y, z = s % YS, s // YS
    links = Links(send, recv)
    tokens = k.shape[0]
    tiles = tokens // TILE

    def at_y(d):
        return z * YS + (y + d) % YS

    def at_z(d):
        return ((z + d) % ZS) * YS + y

    right, left = at_y(1), at_y(3)
    yr, yo, yl = (y + 1) % YS, (y + 2) % YS, (y + 3) % YS
    far_first = (4, 3, 5, 2, 6, 1, 7)
    top, low = pl.ds(0, 128), pl.ds(128, 128)

    def tile(i):
        return pl.ds(i * TILE, TILE)

    loads = [pltpu.make_async_copy(basis, v0, load.at[tiles])]
    for i in range(tiles):
        loads.append(pltpu.make_async_copy(keys.at[0, tile(i)], raw.at[tile(i)], load.at[i]))
    for copy in loads:
        copy.start()
    greet(
        [{"tp": 1 - c}]
        + [{"seq": at_y(d)} for d in range(1, YS)]
        + [{"seq": at_z(d)} for d in range(1, ZS)]
        + [{"req": (x + d) % 4} for d in range(1, 4)]
    )

    loads[0].wait()
    swaps = []
    for i in range(tiles):
        loads[1 + i].wait()
        k[tile(i), :] = raw[tile(i)].reshape(TILE, k.shape[1])
        p_own[tile(i), :] = jnp.dot(k[tile(i), :], v0[...], preferred_element_type=F32)
        swaps.append(links.start(p_own.at[tile(i)], z_in.at[tile(i)], tp=1 - c))
    for i in range(tiles):
        swaps[i].wait_recv()
        zt[:, tile(i)] = (p_own[tile(i), :] + z_in[tile(i), :]).T.astype(B16)
    links.drain()

    for it in range(ITERS):
        run = {}

        def moment(q, j):
            cols = pl.ds(pl.multiple_of(q * (CHUNKS * FEATS) + j * FEATS, FEATS), FEATS)
            return jnp.dot(zt[...], k[:, cols], preferred_element_type=F32)

        def stage0(j):
            opp[j] = moment(yo, j).astype(B16)
            run["r1", j] = links.start(opp.at[j, top], in_a.at[it, j], seq=right)
            run["l1", j] = links.start(opp.at[j, low], in_b.at[it, j], seq=left)
            value = moment(yr, j)
            right32[j] = value[:128]
            right16[j, 128:, :] = value[128:].astype(B16)
            run["r2b", j] = links.start(
                right16.at[j, low], from_left.at[it, j, low], seq=right
            )
            value = moment(yl, j)
            left32[j] = value[128:]
            left16[j, :128, :] = value[:128].astype(B16)
            run["l2a", j] = links.start(left16.at[j, top], from_right.at[it, j, top], seq=left)
            own[j] = moment(y, j)

        def stage1(j):
            run["r1", j].wait_recv()
            right16[j, :128, :] = (right32[j] + in_a[it, j].astype(F32)).astype(B16)
            run["r2a", j] = links.start(
                right16.at[j, top], from_left.at[it, j, top], seq=right
            )
            run["l1", j].wait_recv()
            left16[j, 128:, :] = (left32[j] + in_b[it, j].astype(F32)).astype(B16)
            run["l2b", j] = links.start(left16.at[j, low], from_right.at[it, j, low], seq=left)

        def stage2(j):
            for name in ("r2b", "l2a", "r2a", "l2b"):
                run[name, j].wait_recv()
            value = own[j] + from_left[it, j].astype(F32) + from_right[it, j].astype(F32)
            own[j] = value
            zsend[j] = value.astype(B16)
            for d in far_first:
                rows = pl.ds(pl.multiple_of((z + d) % ZS * PIECE, PIECE), PIECE)
                run["zs", d, j] = links.start(
                    zsend.at[j, rows], zin.at[it, j, d - 1], seq=at_z(d)
                )

        def stage3(j):
            mine = pl.ds(pl.multiple_of(z * PIECE, PIECE), PIECE)
            total = own[j, mine, :]
            for d in far_first:
                run["zs", d, j].wait_recv()
            for d in range(1, ZS):
                total = total + zin[it, j, d - 1].astype(F32)
            full[it, y, j, mine, :] = total.astype(B16)
            for d in far_first:
                run["zg", d, j] = links.start(
                    full.at[it, y, j, mine], full.at[it, y, j, mine], seq=at_z(d)
                )

        def pass_on(q, j, half, to):
            return links.start(full.at[it, q, j, half], full.at[it, q, j, half], seq=to)

        def absorb(q, j, start=False):
            block = full[it, q, j]
            cols = pl.ds(pl.multiple_of(q * (CHUNKS * FEATS) + j * FEATS, FEATS), FEATS)
            product = dot_nt(block, block)
            g_own[...] = product if start else g_own[...] + product
            for i in range(tiles):
                product = dot_nt(k[tile(i), cols], block)
                p_own[tile(i), :] = product if start else p_own[tile(i), :] + product

        def stage4(j):
            for d in far_first:
                run["zg", d, j].wait_recv()
            run["ra", j] = pass_on(y, j, top, right)
            run["lb", j] = pass_on(y, j, low, left)
            run["rb", j] = pass_on(y, j, low, right)
            run["la", j] = pass_on(y, j, top, left)
            absorb(y, j, start=j == 0)

        def stage5(j):
            run["ra", j].wait_recv()
            run["fa", j] = pass_on(yl, j, top, right)
            run["lb", j].wait_recv()
            run["fb", j] = pass_on(yr, j, low, left)

        def stage6(j):
            run["rb", j].wait_recv()
            absorb(yl, j)
            run["la", j].wait_recv()
            absorb(yr, j)

        def stage7(j):
            run["fa", j].wait_recv()
            run["fb", j].wait_recv()
            absorb(yo, j)

        stages = (stage0, stage1, stage2, stage3, stage4, stage5, stage6, stage7)
        for step in range(CHUNKS + len(stages) - 1):
            for at, stage in enumerate(stages):
                if 0 <= step - at < CHUNKS:
                    stage(step - at)

        swap = links.start(g_own, g_in.at[it], tp=1 - c)
        swaps = [
            links.start(p_own.at[tile(i)], p_in.at[it, tile(i)], tp=1 - c) for i in range(tiles)
        ]
        swap.wait_recv()
        invert_factor(g_own[...] + g_in[it], winv, state)
        for copy in swaps:
            copy.wait_recv()
        if it < ITERS - 1:
            for i in range(tiles):
                both = p_own[tile(i), :] + p_in[it, tile(i), :]
                zt[:, tile(i)] = dot_nt(winv[...], both, precision=HI).astype(B16)
            links.drain()

    half = winv[pl.ds(pl.multiple_of(c * 128, 128), 128), :]
    per_tile = TILE // 64
    for i in range(tiles):
        both = p_own[tile(i), :] + p_in[ITERS - 1, tile(i), :]
        rounded = dot_nt(both, half, precision=HI).astype(B16)
        for b in range(per_tile):
            coef[i * per_tile + b] = rounded[64 * b : 64 * b + 64, :]
    for slot in range(16):
        outbox[slot // 4, 64 * (slot % 4) : 64 * (slot % 4) + 64, :] = coef[order[slot]]
    away = [
        (d, links.start(outbox.at[(x + d) % 4], halves.at[c, x], req=(x + d) % 4))
        for d in (2, 1, 3)
    ]
    halves[c, x] = outbox[x]
    across = [links.start(halves.at[c, x], halves.at[c, x], tp=1 - c)]
    for d, copy in away:
        copy.wait_recv()
        r = (x + 4 - d) % 4
        across.append(links.start(halves.at[c, r], halves.at[c, r], tp=1 - c))
    for copy in across:
        copy.wait_recv()
    for r in range(4):
        out[r, :, :128] = halves[0, r]
        out[r, :, 128:] = halves[1, r]
    links.drain()


def subspace_call(order, keys, basis):
    tokens, width = keys.shape[1], basis.shape[0]
    vm = pltpu.VMEM
    wide = (tokens, 256)
    return pl.pallas_call(
        subspace_kernel,
        out_shape=jax.ShapeDtypeStruct((4, 256, 256), B16),
        in_specs=[
            pl.BlockSpec(memory_space=pltpu.SMEM),
            pl.BlockSpec(memory_space=pl.ANY),
            pl.BlockSpec(memory_space=pl.ANY),
        ],
        out_specs=pl.BlockSpec(memory_space=vm),
        scratch_shapes=[
            vm(keys.shape[1:], B16),
            vm((tokens, width), B16),
            vm((width, 256), B16),
            vm((256, tokens), B16),
            vm(wide, F32),
            vm(wide, F32),
            vm((ITERS,) + wide, F32),
            vm((CHUNKS, 256, FEATS), B16),
            vm((CHUNKS, 128, FEATS), F32),
            vm((CHUNKS, 128, FEATS), F32),
            vm((CHUNKS, 256, FEATS), B16),
            vm((CHUNKS, 256, FEATS), B16),
            vm((CHUNKS, 256, FEATS), F32),
            vm((CHUNKS, 256, FEATS), B16),
            vm((ITERS, CHUNKS, 128, FEATS), B16),
            vm((ITERS, CHUNKS, 128, FEATS), B16),
            vm((ITERS, CHUNKS, 256, FEATS), B16),
            vm((ITERS, CHUNKS, 256, FEATS), B16),
            vm((ITERS, CHUNKS, ZS - 1, PIECE, FEATS), B16),
            vm((ITERS, YS, CHUNKS, 256, FEATS), B16),
            vm((256, 256), F32),
            vm((ITERS, 256, 256), F32),
            vm((256, 256), F32),
            vm((256, 256), F32),
            vm((16, 64, 128), B16),
            vm((4, 256, 128), B16),
            vm((2, 4, 256, 128), B16),
            pltpu.SemaphoreType.DMA((tokens // TILE + 1,)),
            pltpu.SemaphoreType.DMA((COPIES,)),
            pltpu.SemaphoreType.DMA((COPIES,)),
        ],
        compiler_params=pltpu.CompilerParams(
            collective_id=0, has_side_effects=True, vmem_limit_bytes=56 * 2**20
        ),
        name="subspace",
    )(order, keys, basis)


def body(keys, start_basis, owner_map):
    rank = start_basis.shape[-1]
    basis = start_basis.reshape(-1, rank)
    owners = owner_map.reshape(-1)
    slots = jnp.arange(owners.shape[0], dtype=jnp.int32)
    order = jnp.sum(jnp.where(owners[None, :] == slots[:, None], slots[None, :], 0), axis=1)
    handed = subspace_call(order, keys, basis)
    return handed[None, None]


def solution(mesh):
    placed = (
        P("req", "seq", None, "tp", None),
        P("req", None, "tp", None, None),
        P("req", "seq", None),
    )
    return jax.shard_map(
        body,
        mesh=mesh,
        in_specs=placed,
        out_specs=P("req", "seq", None, None, None),
        check_vma=False,
    )
```

time: 598 us -> 122 us (0.20)
  waiting for transfers between devices: 363 us -> 0 us
  Pallas kernels: 0 us -> 119 us
  other arithmetic: 119 us -> 1.28 us
  matrix products: 36 us -> 0 us
  blocking collectives: 34.6 us -> 0 us
  local copies, waits for them, and re-layouts: 21.7 us -> 1.87 us
  between operations: 17.4 us -> 0.01 us
    psum x4 -> x0, waiting for transfers between devices: 363 us -> none  [the longest x2 301 us: body(): moment = lax.psum(moment_product(key_rows, projected), 'seq')]
    pallas_call x0 -> x1, Pallas kernels: none -> 119 us  [subspace_call(): pl.pallas_call(subspace_kernel, out_shape=jax.ShapeDtypeStruct((4, 256, 2...]
    another operation x18 -> x0, other arithmetic: 112 us -> none  [the longest x13 68.8 us: orthonormalize(): factor = jnp.linalg.cholesky(shifted)]
    dot_general x8 -> x0, matrix products: 25.4 us -> none  [the longest x2 9.59 us: moment_product(): lax.dot_general(key_cols, coefficients, (((0,), (0,)), ((), ())), preferr...]
    psum x3 -> x0, blocking collectives: 22.1 us -> none  [sum_heads(): return lax.psum(partial_value, 'tp')]
    all_to_all x1 -> x0, blocking collectives: 12.5 us -> none  [body(): lax.all_to_all(placed, 'req', split_axis=0, concat_axis=0, tiled=True)]
    another operation x10 -> x0, matrix products: 10.5 us -> none  [the longest x6 6.23 us: orthonormalize(): return jax.scipy.linalg.solve_triangular(factor, moment.T, lower=True).T]
    reshape x3 -> x0, local copies, waits for them, and re-layouts: 8.37 us -> none  [the longest x1 7.88 us: body(): key_rows = keys.reshape(tokens, -1)]
  transfers between devices with their start and end apart: 4 -> 0, of which waited for: 4 -> 0; matrix products, arithmetic and copies ran while one was open for 0% -> 0% of each run, Pallas kernels for 0% -> 0%
where the time goes in v2:
time: 122 us
  Pallas kernels  119 us (98%)
  local copies, waits for them, and re-layouts  1.87 us (2%)
  other arithmetic  1.28 us (1%)
    pallas_call x1, Pallas kernels, subspace_call(): pl.pallas_call(subspace_kernel, out_shape=jax.ShapeDtypeStruct((4, 256, 2...  119 us

profile of v2, /device:TPU:1, one launch (start us, length us, event | category | flops | bytes accessed | tf_op | source)
XLA Modules:
  0.0 122.1 jit_solution(5502794986616077424)
XLA Ops:
  0.0 1.3 %select_reduce_fusion.order = s32[16]{0:T(128)} fusion(s32[16]{0:T(128)} %bitcast.5), kind=kLoop, calls=%fused_computation | loop fusion | flops 752 | bytes 128 | tf_op jit(solution)/shard_map/reduce_sum | solution.py:371
  1.3 119.0 %subspace.1 = bf16[4,256,256]{2,1,0:T(8,128)(2,1)} custom-call(s32[16]{0:T(128)} %select_reduce_fusion.order, bf16[1,1024,4,4,128]{4,3,2,1,0:T(4,128)(2,1)} %keys.1, bf16[2048,256]{1,0:T(8,128)(2,1)} %bitcast.4), custom_call_target="tpu_custom_call" | custom-call | tf_op jit(solution)/shard_map/subspace/pallas_call | solution.py:318
  120.3 1.9 %copy.5 = bf16[1,1,4,256,256]{4,3,2,1,0:T(8,128)(2,1)} copy(bf16[1,1,4,256,256]{4,3,2,1,0:T(8,128)(2,1)} %bitcast.3) | data formatting | bytes 1048576

commit v3 on v0

v3 whole, which is shorter than its diff:
```python
import jax
import jax.numpy as jnp
from jax import lax
from jax.experimental import pallas as pl
from jax.experimental.pallas import tpu as pltpu
from jax.sharding import PartitionSpec as P

MESH = pl.DeviceIdType.MESH
HI = lax.Precision.HIGHEST
F32 = jnp.float32
B16 = jnp.bfloat16
YS, ZS = 4, 8
ITERS = 2
TILE = 256
RANK = 256
CHUNKS = 4
B = RANK // CHUNKS
WIDE = 512
EVENTS = 4 + ITERS * (CHUNKS * 8 + 2) + 4
VMEM = 53 * 2**20

PLAN = (
    (0, 0, 0), (0, 0, 1), (0, 1, 0), (0, 0, 2), (0, 1, 1), (0, 0, 3), (0, 2, 0), (0, 1, 2),
    (0, 2, 1), (0, 1, 3), (0, 3, 0), (0, 2, 2), (0, 3, 1), (0, 2, 3), (0, 4, 0), (0, 5, 0),
    (0, 3, 2), (0, 4, 1), (0, 5, 1), (0, 3, 3), (0, 4, 2), (0, 8, 0), (0, 5, 2), (0, 9, 0),
    (0, 6, 0), (0, 7, 0), (1, 0, 0), (0, 4, 3), (0, 5, 3), (0, 6, 1), (0, 7, 1), (1, 0, 1),
    (0, 6, 2), (1, 1, 0), (0, 7, 2), (1, 0, 2), (0, 6, 3), (1, 1, 1), (0, 7, 3), (1, 0, 3),
    (1, 2, 0), (1, 1, 2), (1, 2, 1), (1, 1, 3), (1, 3, 0), (1, 2, 2), (1, 3, 1), (1, 2, 3),
    (1, 4, 0), (1, 5, 0), (1, 3, 2), (1, 4, 1), (1, 5, 1), (1, 3, 3), (1, 4, 2), (1, 5, 2),
    (1, 8, 0), (1, 9, 0), (1, 6, 0), (1, 7, 0), (1, 4, 3), (1, 5, 3), (1, 6, 1), (1, 7, 1),
    (1, 6, 2), (1, 7, 2), (1, 6, 3), (1, 7, 3),
)

def dot_nt(a, b, precision=None):
    return lax.dot_general(
        a, b, (((1,), (1,)), ((), ())), precision=precision, preferred_element_type=F32
    )


def dot_tn(a, b, precision=None):
    return lax.dot_general(
        a, b, (((0,), (0,)), ((), ())), precision=precision, preferred_element_type=F32
    )


def eliminate(block):
    b = block.shape[0]
    low = block
    done = []
    sub = lax.broadcasted_iota(jnp.int32, (8, 128), 0)

    def spread(v, j):
        return jnp.broadcast_to(v[j : j + 1, :], (8, 128))

    def columns(rows, first):
        shape = (rows.shape[0], 128)
        return [jnp.broadcast_to(rows[:, first + j : first + j + 1], shape) for j in range(8)]

    for p in range(b // 8):
        head, low = low[:8], low[8:]
        cols = columns(head, 8 * p)
        below = columns(low, 8 * p) if low.shape[0] else None
        for j in range(0, 8, 2):
            a, edge, d = spread(cols[j], j), spread(cols[j], j + 1), spread(cols[j + 1], j + 1)
            root0 = lax.rsqrt(a)
            inv0 = root0 * root0
            ratio = edge * inv0
            root1 = lax.rsqrt(d - ratio * edge)
            inv1 = root1 * root1
            row0, row1 = spread(head, j), spread(head, j + 1)
            row1 = row1 - ratio * row0
            after = range(j + 2, 8)
            tops0 = {m: spread(cols[m], j) for m in after}
            tops1 = {m: spread(cols[m], j + 1) - ratio * tops0[m] for m in after}
            f0 = jnp.where(sub > j + 1, cols[j] * inv0, 0.0)
            f1 = jnp.where(sub > j + 1, (cols[j + 1] - ratio * cols[j]) * inv1, 0.0)
            head = head - f0 * row0 - f1 * row1
            head = jnp.where(sub == j, row0 * root0, head)
            head = jnp.where(sub == j + 1, row1 * root1, head)
            for m in after:
                cols[m] = cols[m] - f0 * tops0[m] - f1 * tops1[m]
            if below:
                g0 = below[j] * inv0[:1]
                g1 = (below[j + 1] - ratio[:1] * below[j]) * inv1[:1]
                low = low - g0 * row0[:1] - g1 * row1[:1]
                for m in after:
                    below[m] = below[m] - g0 * tops0[m][:1] - g1 * tops1[m][:1]
        done.append(head)
    return jnp.concatenate(done, axis=0)[:, b:]


class Links:
    def __init__(self, send, recv, rows):
        self.send, self.recv, self.rows = send, recv, rows
        self.events, self.bytes, self.sent = {}, [], []

    def start(self, event, src, dst, **device):
        i = self.events.setdefault(event, len(self.events))
        if i == len(self.bytes):
            self.bytes.append(0)
        group = event[0]
        while len(self.sent) <= group:
            self.sent.append(0)
        copy = pltpu.make_async_remote_copy(
            src_ref=src,
            dst_ref=dst,
            send_sem=self.send.at[group],
            recv_sem=self.recv.at[i],
            device_id=device,
            device_id_type=MESH,
        )
        copy.start()
        size = 1
        for extent in src.shape:
            size *= extent
        size *= jnp.dtype(src.dtype).itemsize
        self.bytes[i] += size
        self.sent[group] += size

    def take(self, sem, size):
        height = size // (self.rows.shape[1] * 4)
        part = self.rows.at[pl.ds(0, height)]
        pltpu.make_async_copy(part, part, sem).wait()

    def wait(self, event):
        i = self.events[event]
        self.take(self.recv.at[i], self.bytes[i])

    def drain(self):
        for group, size in enumerate(self.sent):
            self.take(self.send.at[group], size)


def greet(partners):
    barrier = pltpu.get_barrier_semaphore()
    for device in partners:
        pl.semaphore_signal(barrier, inc=1, device_id=device, device_id_type=MESH)


def await_greetings(count):
    pl.semaphore_wait(pltpu.get_barrier_semaphore(), count)


def dot3(a, b):
    ah, bh = a.astype(B16), b.astype(B16)
    al, bl = (a - ah.astype(F32)).astype(B16), (b - bh.astype(F32)).astype(B16)

    def dot(p, q):
        return jnp.dot(p, q, preferred_element_type=F32)

    return dot(ah, bh) + (dot(ah, bl) + dot(al, bh))


def subspace_kernel(
    owners, keys, basis, out,
    raw, k, v0, zt, z_own, z_in, pt, pt_in, opp, right16, left16, own, zsend,
    from_left, from_right, from_far, zin, full, squares, sq_send, sq_yin, sq_tin, trace,
    g_own, g_in, winv, coef, outbox, halves, tally, load, send, recv,
):
    x = lax.axis_index("req")
    s = lax.axis_index("seq")
    c = lax.axis_index("tp")
    y, z = s % YS, s // YS
    links = Links(send, recv, tally)
    tokens = k.shape[0]
    tiles = tokens // TILE

    def at_y(d):
        return z * YS + (y + d) % YS

    def at_z(d):
        return ((z + d) % ZS) * YS + y

    right, left = at_y(1), at_y(3)
    yr, yo, yl = (y + 1) % YS, (y + 2) % YS, (y + 3) % YS
    far_first = (4, 3, 5, 2, 6, 1, 7)

    def tile(i):
        return pl.ds(i * TILE, TILE)

    def piece(d):
        p = (z + d) % ZS
        rows = pl.ds(pl.multiple_of(p // 2 * 16, 16), 16)
        return rows, pl.ds(pl.multiple_of(p % 2 * 256, 256), 256)

    partners = (
        [{"tp": 1 - c}]
        + [{"seq": at_y(d)} for d in range(1, YS)]
        + [{"seq": at_z(d)} for d in range(1, ZS)]
        + [{"req": (x + d) % 4} for d in range(1, 4)]
    )
    loads = [pltpu.make_async_copy(basis, v0, load.at[tiles])]
    for i in range(tiles):
        loads.append(pltpu.make_async_copy(keys.at[0, tile(i)], raw.at[tile(i)], load.at[i]))
    for copy in loads:
        copy.start()
    greet(partners)
    order = {}
    for d in range(4):
        for slot in range(4):
            wanted = (x + d) % 4 * 4 + slot
            block = jnp.int32(0)
            for b in range(16):
                block = jnp.where(owners[b] == wanted, b, block)
            order[d, slot] = block

    loads[0].wait()
    for i in range(tiles):
        loads[1 + i].wait()
        k[tile(i), :] = raw[tile(i)].reshape(TILE, k.shape[1])
        z_own[i] = jnp.dot(k[tile(i), :], v0[...], preferred_element_type=F32)
    await_greetings(len(partners))
    for i in range(tiles):
        links.start((0, "z", i), z_own.at[i], z_in.at[i], tp=1 - c)
    for i in range(tiles):
        links.wait((0, "z", i))
        zt[0, :, tile(i)] = (z_own[i] + z_in[i]).T.astype(B16)

    def iteration(it):
        def cols(q):
            return pl.ds(pl.multiple_of(q * WIDE, WIDE), WIDE)

        def moment(q, j):
            return jnp.dot(
                zt[it, B * j : B * j + B, :], k[:, cols(q)], preferred_element_type=F32
            )

        def start(name, j, src, dst, **device):
            links.start((1 + it, name, j), src, dst, **device)

        def wait(name, j):
            links.wait((1 + it, name, j))

        def reduce0(j):
            opp[it, j] = moment(yo, j).astype(B16)
            start("y", j, opp.at[it, j], from_far.at[it, j], seq=at_y(2))
            right16[it, j] = moment(yr, j).astype(B16)
            start("y", j, right16.at[it, j], from_left.at[it, j], seq=right)
            left16[it, j] = moment(yl, j).astype(B16)
            start("y", j, left16.at[it, j], from_right.at[it, j], seq=left)
            own[j] = moment(y, j)

        def reduce1(j):
            wait("y", j)
            value = own[j] + from_far[it, j].astype(F32)
            value = value + from_left[it, j].astype(F32) + from_right[it, j].astype(F32)
            own[j] = value
            zsend[it, j] = value.astype(B16)
            for d in far_first:
                rows, lanes = piece(d)
                start("z", j, zsend.at[it, j, rows, lanes], zin.at[it, j, d - 1], seq=at_z(d))

        def reduce2(j):
            rows, lanes = piece(0)
            total = own[j, rows, lanes]
            wait("z", j)
            for d in range(1, ZS):
                total = total + zin[it, j, d - 1].astype(F32)
            full[it, j, y, rows, lanes] = total.astype(B16)
            for d in far_first:
                mine = full.at[it, j, y, rows, lanes]
                start("gz", j, mine, mine, seq=at_z(d))

        def absorb(q, j, start=False):
            block = full[it, j, q]
            for i in range(tiles):
                product = dot_nt(block, k[tile(i), cols(q)])
                pt[it, j, :, tile(i)] = product if start else pt[it, j, :, tile(i)] + product
            known = jnp.concatenate([full[it, i, q] for i in range(j + 1)], axis=0)
            product = dot_nt(block, known)
            if j < CHUNKS - 1:
                blank = jnp.zeros((B, RANK - B * (j + 1)), F32)
                product = jnp.concatenate([product, blank], axis=1)
            g_own[it, j] = product if start else g_own[it, j] + product

        def gather0(j):
            wait("gz", j)
            power = jnp.square(full[it, j, y].astype(F32))
            power = jnp.sum(power.reshape(B // 8, 8, WIDE), axis=0)
            power = sum(power[:, 128 * g : 128 * g + 128] for g in range(WIDE // 128))
            squares[it] = power if j == 0 else squares[it] + power
            if j == CHUNKS - 1:
                for d in (2, 1, 3):
                    start("ty", 0, squares.at[it], sq_yin.at[it, d - 1], seq=at_y(d))
            mine = full.at[it, j, y]
            start("go", j, mine, mine, seq=at_y(2))
            start("gr", j, mine, mine, seq=right)
            start("gl", j, mine, mine, seq=left)
            absorb(y, j, start=True)

        def gather1(j):
            wait("gr", j)
            absorb(yl, j)
            wait("gl", j)
            absorb(yr, j)

        def gather2(j):
            wait("go", j)
            absorb(yo, j)
            start("g", j, g_own.at[it, j], g_in.at[it, j], tp=1 - c)
            start("p", j, pt.at[it, j], pt_in.at[it, j], tp=1 - c)

        def trace1(_):
            total = squares[it]
            wait("ty", 0)
            for d in range(1, YS):
                total = total + sq_yin[it, d - 1]
            sq_send[it] = total
            start("tt", 0, sq_send.at[it], sq_tin.at[it], tp=1 - c)

        def trace2(_):
            wait("tt", 0)
            trace[it] = sq_send[it] + sq_tin[it]

        def factor(j):
            lo = B * j
            wait("g", j)
            gram = g_own[it, j] + g_in[it, j]
            shift = 0.0001 * jnp.sum(trace[it]) / RANK
            r = lax.broadcasted_iota(jnp.int32, (B, B), 0)
            l = lax.broadcasted_iota(jnp.int32, (B, B), 1)
            eye = jnp.where(r == l, 1.0, 0.0).astype(F32)
            corner = gram[:, lo : lo + B] + shift * eye
            if j:
                lane = lax.broadcasted_iota(jnp.int32, (B, RANK), 1)
                before = winv[:lo, :]
                row = dot_nt(jnp.where(lane < lo, gram, 0.0), before, precision=HI)
                corner = corner - dot_nt(row, row, precision=HI)
                back = jnp.dot(row, before, precision=HI, preferred_element_type=F32)
            inverse = eliminate(jnp.concatenate([corner, eye], axis=1))
            parts = [jnp.zeros((B, lo), F32)] if lo else []
            parts.append(inverse)
            if lo + B < RANK:
                parts.append(jnp.zeros((B, RANK - lo - B), F32))
            rows = jnp.concatenate(parts, axis=1)
            if j:
                rows = rows - jnp.dot(
                    inverse, back, precision=HI, preferred_element_type=F32
                )
            winv[lo : lo + B, :] = rows

        def project(j):
            wait("p", j)
            pt_in[it, j] = pt[it, j] + pt_in[it, j]
            if it < ITERS - 1:
                known = jnp.concatenate([pt_in[it, i] for i in range(j + 1)], axis=0)
                rows = winv[B * j : B * j + B, : B * (j + 1)]
                zt[it + 1, B * j : B * j + B, :] = dot3(rows, known).astype(B16)

        return (
            reduce0, reduce1, reduce2, gather0, gather1, gather2, factor, project,
            trace1, trace2,
        )

    steps = [iteration(it) for it in range(ITERS)]
    for it, step, j in PLAN:
        steps[it][step](j)

    half = winv[pl.ds(pl.multiple_of(c * 128, 128), 128), :]
    per_tile = TILE // 64
    for i in range(tiles):
        both = jnp.concatenate([pt_in[ITERS - 1, j, :, tile(i)] for j in range(CHUNKS)], axis=0)
        rounded = dot3(half, both).T.astype(B16)
        for b in range(per_tile):
            coef[i * per_tile + b] = rounded[64 * b : 64 * b + 64, :]
    last = 1 + ITERS
    for d in (2, 1, 3, 0):
        rows = jnp.concatenate([coef[order[d, slot]] for slot in range(4)], axis=0)
        if d:
            outbox[d - 1] = rows
            there = halves.at[c, x]
            links.start((last, "x", d), outbox.at[d - 1], there, req=(x + d) % 4)
        else:
            halves[c, x] = rows
    for d in (0, 2, 1, 3):
        r = (x + 4 - d) % 4
        if d:
            links.wait((last, "x", d))
        links.start((last, "c", 0), halves.at[c, r], halves.at[c, r], tp=1 - c)
    links.wait((last, "c", 0))
    for r in range(4):
        out[r, :, :128] = halves[0, r]
        out[r, :, 128:] = halves[1, r]
    links.drain()


def subspace_call(owners, keys, basis):
    tokens, width = keys.shape[1], basis.shape[0]
    vm = pltpu.VMEM
    tiles = tokens // TILE
    every = (ITERS, CHUNKS)
    return pl.pallas_call(
        subspace_kernel,
        out_shape=jax.ShapeDtypeStruct((4, 256, 256), B16),
        in_specs=[
            pl.BlockSpec(memory_space=pltpu.SMEM),
            pl.BlockSpec(memory_space=pl.ANY),
            pl.BlockSpec(memory_space=pl.ANY),
        ],
        out_specs=pl.BlockSpec(memory_space=vm),
        scratch_shapes=[
            vm(keys.shape[1:], B16),
            vm((tokens, width), B16),
            vm((width, RANK), B16),
            vm((ITERS, RANK, tokens), B16),
            vm((tiles, TILE, RANK), F32),
            vm((tiles, TILE, RANK), F32),
            vm(every + (B, tokens), F32),
            vm(every + (B, tokens), F32),
            vm(every + (B, WIDE), B16),
            vm(every + (B, WIDE), B16),
            vm(every + (B, WIDE), B16),
            vm((CHUNKS, B, WIDE), F32),
            vm(every + (B, WIDE), B16),
            vm(every + (B, WIDE), B16),
            vm(every + (B, WIDE), B16),
            vm(every + (B, WIDE), B16),
            vm(every + (ZS - 1, 16, 256), B16),
            vm(every + (YS, B, WIDE), B16),
            vm((ITERS, 8, 128), F32),
            vm((ITERS, 8, 128), F32),
            vm((ITERS, YS - 1, 8, 128), F32),
            vm((ITERS, 8, 128), F32),
            vm((ITERS, 8, 128), F32),
            vm(every + (B, RANK), F32),
            vm(every + (B, RANK), F32),
            vm((RANK, RANK), F32),
            vm((16, 64, 128), B16),
            vm((3, 256, 128), B16),
            vm((2, 4, 256, 128), B16),
            vm((8192, 128), F32),
            pltpu.SemaphoreType.DMA((tiles + 1,)),
            pltpu.SemaphoreType.DMA((2 + ITERS,)),
            pltpu.SemaphoreType.DMA((EVENTS,)),
        ],
        compiler_params=pltpu.CompilerParams(
            collective_id=0, has_side_effects=True, vmem_limit_bytes=VMEM
        ),
        name="subspace",
    )(owners, keys, basis)


def body(keys, start_basis, owner_map):
    basis = start_basis.reshape(-1, start_basis.shape[-1])
    handed = subspace_call(owner_map.reshape(-1), keys, basis)
    return handed[None, None]


def solution(mesh):
    placed = (
        P("req", "seq", None, "tp", None),
        P("req", None, "tp", None, None),
        P("req", "seq", None),
    )
    return jax.shard_map(
        body,
        mesh=mesh,
        in_specs=placed,
        out_specs=P("req", "seq", None, None, None),
        check_vma=False,
    )
```

time: 598 us -> 104 us (0.17)
  waiting for transfers between devices: 363 us -> 0 us
  other arithmetic: 119 us -> 0 us
  Pallas kernels: 0 us -> 103 us
  matrix products: 36 us -> 0 us
  blocking collectives: 34.6 us -> 0 us
  local copies, waits for them, and re-layouts: 21.7 us -> 1.45 us
  between operations: 17.4 us -> 0.01 us
    psum x4 -> x0, waiting for transfers between devices: 363 us -> none  [the longest x2 301 us: body(): moment = lax.psum(moment_product(key_rows, projected), 'seq')]
    another operation x18 -> x0, other arithmetic: 112 us -> none  [the longest x13 68.8 us: orthonormalize(): factor = jnp.linalg.cholesky(shifted)]
    pallas_call x0 -> x1, Pallas kernels: none -> 103 us  [subspace_call(): pl.pallas_call(subspace_kernel, out_shape=jax.ShapeDtypeStruct((4, 256, 2...]
    dot_general x8 -> x0, matrix products: 25.4 us -> none  [the longest x2 9.59 us: moment_product(): lax.dot_general(key_cols, coefficients, (((0,), (0,)), ((), ())), preferr...]
    psum x3 -> x0, blocking collectives: 22.1 us -> none  [sum_heads(): return lax.psum(partial_value, 'tp')]
    all_to_all x1 -> x0, blocking collectives: 12.5 us -> none  [body(): lax.all_to_all(placed, 'req', split_axis=0, concat_axis=0, tiled=True)]
    another operation x10 -> x0, matrix products: 10.5 us -> none  [the longest x6 6.23 us: orthonormalize(): return jax.scipy.linalg.solve_triangular(factor, moment.T, lower=True).T]
    reshape x3 -> x0, local copies, waits for them, and re-layouts: 8.37 us -> none  [the longest x1 7.88 us: body(): key_rows = keys.reshape(tokens, -1)]
  transfers between devices with their start and end apart: 4 -> 0, of which waited for: 4 -> 0; matrix products, arithmetic and copies ran while one was open for 0% -> 0% of each run, Pallas kernels for 0% -> 0%
where the time goes in v3:
time: 104 us
  Pallas kernels  103 us (99%)
  local copies, waits for them, and re-layouts  1.45 us (1%)
    pallas_call x1, Pallas kernels, subspace_call(): pl.pallas_call(subspace_kernel, out_shape=jax.ShapeDtypeStruct((4, 256, 2...  103 us

profile of v3, /device:TPU:1, one launch (start us, length us, event | category | flops | bytes accessed | tf_op | source)
XLA Modules:
  0.0 104.2 jit_solution(9074644262540845670)
XLA Ops:
  0.0 0.0 copy-start
  0.0 0.7 copy-done
  0.7 102.8 %subspace.1 = bf16[4,256,256]{2,1,0:T(8,128)(2,1)S(1)} custom-call(s32[16]{0:T(128)S(1)} %bitcast.4, bf16[1,1024,4,4,128]{4,3,2,1,0:T(4,128)(2,1)} %keys.1, bf16[2048,256]{1,0:T(8,128)(2,1)} %bitcast.5), custom_call_target="tpu_custom_call" | custom-call | tf_op jit(solution)/shard_map/subspace/pallas_call | solution.py:392
  103.4 0.8 copy.5
Async XLA Ops:
  0.0 0.7 copy-start

commit v4 on v3

--- a/solution.py
+++ b/solution.py
@@ -16,19 +16,20 @@
 CHUNKS = 4
 B = RANK // CHUNKS
 WIDE = 512
-EVENTS = 4 + ITERS * (CHUNKS * 8 + 2) + 4
+EVENTS = 4 + ITERS * (CHUNKS * 8 + 2) + 8
 VMEM = 53 * 2**20
 
 PLAN = (
-    (0, 0, 0), (0, 0, 1), (0, 1, 0), (0, 0, 2), (0, 1, 1), (0, 0, 3), (0, 2, 0), (0, 1, 2),
-    (0, 2, 1), (0, 1, 3), (0, 3, 0), (0, 2, 2), (0, 3, 1), (0, 2, 3), (0, 4, 0), (0, 5, 0),
-    (0, 3, 2), (0, 4, 1), (0, 5, 1), (0, 3, 3), (0, 4, 2), (0, 8, 0), (0, 5, 2), (0, 9, 0),
-    (0, 6, 0), (0, 7, 0), (1, 0, 0), (0, 4, 3), (0, 5, 3), (0, 6, 1), (0, 7, 1), (1, 0, 1),
-    (0, 6, 2), (1, 1, 0), (0, 7, 2), (1, 0, 2), (0, 6, 3), (1, 1, 1), (0, 7, 3), (1, 0, 3),
-    (1, 2, 0), (1, 1, 2), (1, 2, 1), (1, 1, 3), (1, 3, 0), (1, 2, 2), (1, 3, 1), (1, 2, 3),
-    (1, 4, 0), (1, 5, 0), (1, 3, 2), (1, 4, 1), (1, 5, 1), (1, 3, 3), (1, 4, 2), (1, 5, 2),
-    (1, 8, 0), (1, 9, 0), (1, 6, 0), (1, 7, 0), (1, 4, 3), (1, 5, 3), (1, 6, 1), (1, 7, 1),
-    (1, 6, 2), (1, 7, 2), (1, 6, 3), (1, 7, 3),
+    (0, 0, 0), (0, 0, 1), (0, 0, 2), (0, 1, 0), (0, 0, 3), (0, 1, 1), (0, 2, 0), (0, 1, 2),
+    (0, 2, 1), (0, 1, 3), (0, 3, 0), (0, 2, 2), (0, 3, 1), (0, 2, 3), (0, 3, 2), (0, 4, 0),
+    (0, 5, 0), (0, 3, 3), (0, 4, 1), (0, 5, 1), (0, 8, 0), (0, 9, 0), (0, 6, 0), (0, 7, 0),
+    (1, 0, 0), (0, 4, 2), (0, 5, 2), (0, 4, 3), (0, 5, 3), (0, 6, 1), (1, 1, 0), (0, 7, 1),
+    (1, 0, 1), (0, 6, 2), (0, 7, 2), (1, 0, 2), (0, 6, 3), (1, 1, 1), (1, 2, 0), (0, 7, 3),
+    (1, 0, 3), (1, 1, 2), (1, 2, 1), (1, 1, 3), (1, 3, 0), (1, 2, 2), (1, 3, 1), (1, 2, 3),
+    (1, 3, 2), (1, 4, 0), (1, 5, 0), (1, 3, 3), (1, 4, 1), (1, 5, 1), (1, 8, 0), (1, 9, 0),
+    (1, 4, 2), (1, 5, 2), (1, 6, 0), (1, 7, 0), (1, 6, 1), (1, 7, 1), (1, 10, 0), (1, 4, 3),
+    (1, 5, 3), (1, 6, 2), (1, 11, 0), (1, 7, 2), (1, 6, 3), (1, 7, 3), (1, 10, 1), (1, 12, 0),
+    (1, 11, 1), (1, 12, 1),
 )
 
 def dot_nt(a, b, precision=None):
@@ -197,24 +198,23 @@
     greet(partners)
     order = {}
     for d in range(4):
-        for slot in range(4):
-            wanted = (x + d) % 4 * 4 + slot
+        for t in range(2):
+            wanted = (x + d) % 4 * 4 + 2 * c + t
             block = jnp.int32(0)
             for b in range(16):
                 block = jnp.where(owners[b] == wanted, b, block)
-            order[d, slot] = block
+            order[d, t] = block
 
     loads[0].wait()
     for i in range(tiles):
         loads[1 + i].wait()
         k[tile(i), :] = raw[tile(i)].reshape(TILE, k.shape[1])
-        z_own[i] = jnp.dot(k[tile(i), :], v0[...], preferred_element_type=F32)
+        value = jnp.dot(k[tile(i), :], v0[...], preferred_element_type=F32).T
+        for j in range(CHUNKS):
+            z_own[j, :, tile(i)] = value[B * j : B * j + B]
     await_greetings(len(partners))
-    for i in range(tiles):
-        links.start((0, "z", i), z_own.at[i], z_in.at[i], tp=1 - c)
-    for i in range(tiles):
-        links.wait((0, "z", i))
-        zt[0, :, tile(i)] = (z_own[i] + z_in[i]).T.astype(B16)
+    for j in range(CHUNKS):
+        links.start((0, "z", j), z_own.at[j], z_in.at[j], tp=1 - c)
 
     def iteration(it):
         def cols(q):
@@ -232,6 +232,9 @@
             links.wait((1 + it, name, j))
 
         def reduce0(j):
+            if it == 0:
+                links.wait((0, "z", j))
+                zt[0, B * j : B * j + B, :] = (z_own[j] + z_in[j]).astype(B16)
             opp[it, j] = moment(yo, j).astype(B16)
             start("y", j, opp.at[it, j], from_far.at[it, j], seq=at_y(2))
             right16[it, j] = moment(yr, j).astype(B16)
@@ -347,40 +350,50 @@
                 rows = winv[B * j : B * j + B, : B * (j + 1)]
                 zt[it + 1, B * j : B * j + B, :] = dot3(rows, known).astype(B16)
 
+        last = 1 + ITERS
+        slots = pl.ds(2 * c, 2)
+
+        def hand0(h):
+            lo, hi = 128 * h, 128 * h + 128
+            rows = winv[lo:hi, :hi]
+            for i in range(tiles):
+                known = [pt_in[it, j, :, tile(i)] for j in range(hi // B)]
+                rounded = dot3(rows, jnp.concatenate(known, axis=0)).T.astype(B16)
+                for b in range(TILE // 64):
+                    coef[h, i * (TILE // 64) + b] = rounded[64 * b : 64 * b + 64, :]
+            for d in (2, 1, 3, 0):
+                for t in range(2):
+                    if d:
+                        outbox[h, d - 1, t] = coef[h, order[d, t]]
+                    else:
+                        halves[h, x, 2 * c + t] = coef[h, order[d, t]]
+                if d:
+                    there = halves.at[h, x, slots]
+                    links.start((last, h, d), outbox.at[h, d - 1], there, req=(x + d) % 4)
+
+        def hand1(h):
+            for d in (0, 2, 1, 3):
+                r = (x + 4 - d) % 4
+                if d:
+                    links.wait((last, h, d))
+                mine = halves.at[h, r, slots]
+                links.start((last, h, 0), mine, mine, tp=1 - c)
+
+        def hand2(h):
+            links.wait((last, h, 0))
+            for r in range(4):
+                for slot in range(4):
+                    out[r, 64 * slot : 64 * slot + 64, 128 * h : 128 * h + 128] = halves[h, r, slot]
+
         return (
             reduce0, reduce1, reduce2, gather0, gather1, gather2, factor, project,
-            trace1, trace2,
+            trace1, trace2, hand0, hand1, hand2,
         )
 
     steps = [iteration(it) for it in range(ITERS)]
     for it, step, j in PLAN:
         steps[it][step](j)
 
-    half = winv[pl.ds(pl.multiple_of(c * 128, 128), 128), :]
-    per_tile = TILE // 64
-    for i in range(tiles):
-        both = jnp.concatenate([pt_in[ITERS - 1, j, :, tile(i)] for j in range(CHUNKS)], axis=0)
-        rounded = dot3(half, both).T.astype(B16)
-        for b in range(per_tile):
-            coef[i * per_tile + b] = rounded[64 * b : 64 * b + 64, :]
-    last = 1 + ITERS
-    for d in (2, 1, 3, 0):
-        rows = jnp.concatenate([coef[order[d, slot]] for slot in range(4)], axis=0)
-        if d:
-            outbox[d - 1] = rows
-            there = halves.at[c, x]
-            links.start((last, "x", d), outbox.at[d - 1], there, req=(x + d) % 4)
-        else:
-            halves[c, x] = rows
-    for d in (0, 2, 1, 3):
-        r = (x + 4 - d) % 4
-        if d:
-            links.wait((last, "x", d))
-        links.start((last, "c", 0), halves.at[c, r], halves.at[c, r], tp=1 - c)
-    links.wait((last, "c", 0))
-    for r in range(4):
-        out[r, :, :128] = halves[0, r]
-        out[r, :, 128:] = halves[1, r]
     links.drain()
 
 
@@ -403,8 +416,8 @@
             vm((tokens, width), B16),
             vm((width, RANK), B16),
             vm((ITERS, RANK, tokens), B16),
-            vm((tiles, TILE, RANK), F32),
-            vm((tiles, TILE, RANK), F32),
+            vm((CHUNKS, B, tokens), F32),
+            vm((CHUNKS, B, tokens), F32),
             vm(every + (B, tokens), F32),
             vm(every + (B, tokens), F32),
             vm(every + (B, WIDE), B16),
@@ -425,9 +438,9 @@
             vm(every + (B, RANK), F32),
             vm(every + (B, RANK), F32),
             vm((RANK, RANK), F32),
-            vm((16, 64, 128), B16),
-            vm((3, 256, 128), B16),
-            vm((2, 4, 256, 128), B16),
+            vm((2, 16, 64, 128), B16),
+            vm((2, 3, 2, 64, 128), B16),
+            vm((2, 4, 4, 64, 128), B16),
             vm((8192, 128), F32),
             pltpu.SemaphoreType.DMA((tiles + 1,)),
             pltpu.SemaphoreType.DMA((2 + ITERS,)),

time: 104 us -> 102 us (0.981)
  Pallas kernels: 103 us -> 101 us
    pallas_call x1, Pallas kernels: 103 us -> 101 us  [subspace_call(): pl.pallas_call(subspace_kernel, out_shape=jax.ShapeDtypeStruct((4, 256, 2...]
where the time goes in v4:
time: 102 us
  Pallas kernels  101 us (99%)
  local copies, waits for them, and re-layouts  1.45 us (1%)
    pallas_call x1, Pallas kernels, subspace_call(): pl.pallas_call(subspace_kernel, out_shape=jax.ShapeDtypeStruct((4, 256, 2...  101 us

profile of v4, /device:TPU:1, one launch (start us, length us, event | category | flops | bytes accessed | tf_op | source)
XLA Modules:
  0.0 102.2 jit_solution(1152581891158011617)
XLA Ops:
  0.0 0.0 copy-start
  0.0 0.7 copy-done
  0.7 100.8 %subspace.1 = bf16[4,256,256]{2,1,0:T(8,128)(2,1)S(1)} custom-call(s32[16]{0:T(128)S(1)} %bitcast.4, bf16[1,1024,4,4,128]{4,3,2,1,0:T(4,128)(2,1)} %keys.1, bf16[2048,256]{1,0:T(8,128)(2,1)} %bitcast.5), custom_call_target="tpu_custom_call" | custom-call | tf_op jit(solution)/shard_map/subspace/pallas_call | solution.py:405
  101.5 0.8 copy.5
Async XLA Ops:
  0.0 0.7 copy-start

commit v5 on v4

--- a/solution.py
+++ b/solution.py
@@ -16,20 +16,19 @@
 CHUNKS = 4
 B = RANK // CHUNKS
 WIDE = 512
-EVENTS = 4 + ITERS * (CHUNKS * 8 + 2) + 8
+EVENTS = 4 + ITERS * (CHUNKS * 8 + 1) + 8
 VMEM = 53 * 2**20
 
 PLAN = (
     (0, 0, 0), (0, 0, 1), (0, 0, 2), (0, 1, 0), (0, 0, 3), (0, 1, 1), (0, 2, 0), (0, 1, 2),
     (0, 2, 1), (0, 1, 3), (0, 3, 0), (0, 2, 2), (0, 3, 1), (0, 2, 3), (0, 3, 2), (0, 4, 0),
-    (0, 5, 0), (0, 3, 3), (0, 4, 1), (0, 5, 1), (0, 8, 0), (0, 9, 0), (0, 6, 0), (0, 7, 0),
-    (1, 0, 0), (0, 4, 2), (0, 5, 2), (0, 4, 3), (0, 5, 3), (0, 6, 1), (1, 1, 0), (0, 7, 1),
-    (1, 0, 1), (0, 6, 2), (0, 7, 2), (1, 0, 2), (0, 6, 3), (1, 1, 1), (1, 2, 0), (0, 7, 3),
-    (1, 0, 3), (1, 1, 2), (1, 2, 1), (1, 1, 3), (1, 3, 0), (1, 2, 2), (1, 3, 1), (1, 2, 3),
-    (1, 3, 2), (1, 4, 0), (1, 5, 0), (1, 3, 3), (1, 4, 1), (1, 5, 1), (1, 8, 0), (1, 9, 0),
-    (1, 4, 2), (1, 5, 2), (1, 6, 0), (1, 7, 0), (1, 6, 1), (1, 7, 1), (1, 10, 0), (1, 4, 3),
-    (1, 5, 3), (1, 6, 2), (1, 11, 0), (1, 7, 2), (1, 6, 3), (1, 7, 3), (1, 10, 1), (1, 12, 0),
-    (1, 11, 1), (1, 12, 1),
+    (0, 5, 0), (0, 3, 3), (0, 4, 1), (0, 5, 1), (0, 8, 0), (0, 6, 0), (0, 7, 0), (1, 0, 0),
+    (0, 4, 2), (0, 5, 2), (0, 4, 3), (0, 5, 3), (0, 6, 1), (1, 1, 0), (0, 7, 1), (1, 0, 1),
+    (0, 6, 2), (0, 7, 2), (1, 0, 2), (0, 6, 3), (1, 1, 1), (1, 2, 0), (0, 7, 3), (1, 0, 3),
+    (1, 1, 2), (1, 2, 1), (1, 1, 3), (1, 3, 0), (1, 2, 2), (1, 3, 1), (1, 2, 3), (1, 3, 2),
+    (1, 4, 0), (1, 5, 0), (1, 3, 3), (1, 4, 1), (1, 5, 1), (1, 8, 0), (1, 4, 2), (1, 5, 2),
+    (1, 6, 0), (1, 7, 0), (1, 6, 1), (1, 7, 1), (1, 9, 0), (1, 4, 3), (1, 5, 3), (1, 6, 2),
+    (1, 10, 0), (1, 7, 2), (1, 6, 3), (1, 7, 3), (1, 9, 1), (1, 11, 0), (1, 10, 1), (1, 11, 1),
 )
 
 def dot_nt(a, b, precision=None):
@@ -155,7 +154,7 @@
 def subspace_kernel(
     owners, keys, basis, out,
     raw, k, v0, zt, z_own, z_in, pt, pt_in, opp, right16, left16, own, zsend,
-    from_left, from_right, from_far, zin, full, squares, sq_send, sq_yin, sq_tin, trace,
+    from_left, from_right, from_far, zin, full, squares, sq_in, trace,
     g_own, g_in, winv, coef, outbox, halves, tally, load, send, recv,
 ):
     x = lax.axis_index("req")
@@ -187,6 +186,7 @@
     partners = (
         [{"tp": 1 - c}]
         + [{"seq": at_y(d)} for d in range(1, YS)]
+        + [{"seq": at_y(d), "tp": 1 - c} for d in range(1, YS)]
         + [{"seq": at_z(d)} for d in range(1, ZS)]
         + [{"req": (x + d) % 4} for d in range(1, 4)]
     )
@@ -283,8 +283,12 @@
             power = sum(power[:, 128 * g : 128 * g + 128] for g in range(WIDE // 128))
             squares[it] = power if j == 0 else squares[it] + power
             if j == CHUNKS - 1:
+                sq_in[it, YS * c + y] = squares[it]
+                there = sq_in.at[it, YS * c + y]
                 for d in (2, 1, 3):
-                    start("ty", 0, squares.at[it], sq_yin.at[it, d - 1], seq=at_y(d))
+                    start("t", 0, squares.at[it], there, seq=at_y(d))
+                    start("t", 0, squares.at[it], there, seq=at_y(d), tp=1 - c)
+                start("t", 0, squares.at[it], there, tp=1 - c)
             mine = full.at[it, j, y]
             start("go", j, mine, mine, seq=at_y(2))
             start("gr", j, mine, mine, seq=right)
@@ -304,16 +308,11 @@
             start("p", j, pt.at[it, j], pt_in.at[it, j], tp=1 - c)
 
         def trace1(_):
-            total = squares[it]
-            wait("ty", 0)
-            for d in range(1, YS):
-                total = total + sq_yin[it, d - 1]
-            sq_send[it] = total
-            start("tt", 0, sq_send.at[it], sq_tin.at[it], tp=1 - c)
-
-        def trace2(_):
-            wait("tt", 0)
-            trace[it] = sq_send[it] + sq_tin[it]
+            wait("t", 0)
+            total = sq_in[it, 0]
+            for i in range(1, 2 * YS):
+                total = total + sq_in[it, i]
+            trace[it] = total
 
         def factor(j):
             lo = B * j
@@ -387,7 +386,7 @@
 
         return (
             reduce0, reduce1, reduce2, gather0, gather1, gather2, factor, project,
-            trace1, trace2, hand0, hand1, hand2,
+            trace1, hand0, hand1, hand2,
         )
 
     steps = [iteration(it) for it in range(ITERS)]
@@ -431,9 +430,7 @@
             vm(every + (ZS - 1, 16, 256), B16),
             vm(every + (YS, B, WIDE), B16),
             vm((ITERS, 8, 128), F32),
-            vm((ITERS, 8, 128), F32),
-            vm((ITERS, YS - 1, 8, 128), F32),
-            vm((ITERS, 8, 128), F32),
+            vm((ITERS, 2 * YS, 8, 128), F32),
             vm((ITERS, 8, 128), F32),
             vm(every + (B, RANK), F32),
             vm(every + (B, RANK), F32),

time: 102 us -> 102 us (level)
  no operation moved by 1% of the time
where the time goes in v5:
time: 102 us
  Pallas kernels  101 us (99%)
  local copies, waits for them, and re-layouts  1.45 us (1%)
    pallas_call x1, Pallas kernels, subspace_call(): pl.pallas_call(subspace_kernel, out_shape=jax.ShapeDtypeStruct((4, 256, 2...  101 us

profile of v5, /device:TPU:1, one launch (start us, length us, event | category | flops | bytes accessed | tf_op | source)
XLA Modules:
  0.0 102.3 jit_solution(2957078814498381589)
XLA Ops:
  0.0 0.0 copy-start
  0.0 0.7 copy-done
  0.7 100.9 %subspace.1 = bf16[4,256,256]{2,1,0:T(8,128)(2,1)S(1)} custom-call(s32[16]{0:T(128)S(1)} %bitcast.4, bf16[1,1024,4,4,128]{4,3,2,1,0:T(4,128)(2,1)} %keys.1, bf16[2048,256]{1,0:T(8,128)(2,1)} %bitcast.5), custom_call_target="tpu_custom_call" | custom-call | tf_op jit(solution)/shard_map/subspace/pallas_call | solution.py:404
  101.5 0.8 copy.5
Async XLA Ops:
  0.0 0.7 copy-start
